TPU v7x, 128 devices: a whole 4x4x4 slice. The times are simulated.
128 devices in a mesh: dp: 128 (over z, y, x, core).
Axes of the slice: x: 4, y: 4, z: 4, core: 2. Of those that a mesh axis runs over, the one named last changes fastest.
Arguments:
- embeddings: bfloat16 [131072, 1024], P('dp')
- partners: int32 [128, 13], P('dp'), may hold values from 0 to 127, as said below
- pair_count: int32 [128], P('dp'), may hold values from 1 to 13, as said below
Outputs:
- soft_cosine: float32 [131072], P('dp')
Inputs may be any that keep to these rules, and one draw needn't show every extreme that they name: Entry 0 of partners[h] is h; the live entries of partners[h] are distinct blocks from h to min(h + 16, 127), so each unordered pair of blocks stands once; entries past pair_count[h] are arbitrary blocks in that range and are not pairs. `pair_count`: at most 13 live pairs for one block; some block has exactly 13.
All inputs are finite; a program needn't handle non-finite values.
Results may differ from a plain program's by a relative error of at most 0.00043.
Values may be sent and summed in bfloat16 or wider, within the bound.
No kernel may reach another device: no remote copies, remote signals or barrier semaphores. Data moves between devices by JAX's collectives and lax.ppermute only.
A program may use at most 128 MiB of HBM per device.

v0:
```python
import functools

import jax
import jax.numpy as jnp
from jax import lax
from jax.experimental import pallas as pl
from jax.experimental.pallas import tpu as pltpu
from jax.sharding import PartitionSpec as P

SCALE = 256.0
LOG2E = 1.4426950408889634
LN2 = 0.6931471805599453
GAIN = SCALE * LOG2E
LEAST = 2.0**-60
MOST = 2.0**112
FLOOR = -1e30
MASKED = -1e27
SCRATCH = 22
PLACES = [(0, 0), (0, 1), (3, 0), (1, 0), (3, 1), (1, 1), (2, 0), (2, 1)]
B = 1024
D = 1024
H = B // 2
CH = 256
G = 32
COUNT = 128
RING = 8
HALVES = B // 2 // CH
LIST = 16
GRANT = 63 * 2**20 + 2**19


def around(dx):
    moves = []
    for d in range(COUNT):
        core, x, rest = d % 2, (d // 2) % 4, d // RING
        moves.append((d, rest * RING + ((x + dx) % 4) * 2 + core))
    return moves


def along(steps, flip=0):
    return [(d, (d + steps) ^ flip) for d in range(COUNT) if 0 <= d + steps < COUNT]


def send(value, moves):
    return lax.ppermute(value, "dp", moves)


def unit_kernel(list_ref, count_ref, x_ref, o_ref, top_ref, low_ref, x, o, in_sem, out_sem):
    def rows(i):
        return pl.ds(i * CH, CH)

    loads = [pltpu.make_async_copy(x_ref.at[rows(i), :], x.at[rows(i), :], in_sem.at[i]) for i in range(B // CH)]
    for load in loads:
        load.start()
    lane = lax.broadcasted_iota(jnp.int32, (LIST, D), 1)
    pairs = jnp.full((LIST, D), -1.0, jnp.float32)
    for k in range(list_ref.shape[1]):
        entry = jnp.where(k < count_ref[0], list_ref[0, k], -1).astype(jnp.float32)
        pairs = jnp.where(lane == k, entry, pairs)
    o[B : B + LIST, :] = pairs.astype(jnp.bfloat16)
    stores = [pltpu.make_async_copy(o.at[pl.ds(B, LIST), :], o_ref.at[pl.ds(B, LIST), :], out_sem.at[0])]
    stores[0].start()
    for i in range(B // CH):
        loads[i].wait()
        for g in range(CH // G):
            at = slice(i * CH + g * G, i * CH + (g + 1) * G)
            v = x[at, :].astype(jnp.float32)
            size = jnp.sum(v * v, -1, keepdims=True)
            o[at, :] = (v * lax.rsqrt(size + 1e-06)).astype(jnp.bfloat16)
        stores.append(pltpu.make_async_copy(o.at[rows(i), :], o_ref.at[rows(i), :], out_sem.at[2 * i + 1]))
        half = top_ref.at[rows(i), :] if i < HALVES else low_ref.at[rows(i - HALVES), :]
        stores.append(pltpu.make_async_copy(o.at[rows(i), :], half, out_sem.at[2 * i + 2]))
        stores[-2].start()
        stores[-1].start()
    for store in stores:
        store.wait()


def normalize(embeddings, partners, pair_count):
    bf16 = jnp.bfloat16
    smem, anywhere = pl.BlockSpec(memory_space=pltpu.SMEM), pl.BlockSpec(memory_space=pl.ANY)
    return pl.pallas_call(
        unit_kernel,
        in_specs=[smem, smem, anywhere],
        out_specs=[anywhere] * 3,
        out_shape=[
            jax.ShapeDtypeStruct((B + LIST, D), bf16),
            jax.ShapeDtypeStruct((B // 2, D), bf16),
            jax.ShapeDtypeStruct((B // 2, D), bf16),
        ],
        scratch_shapes=[
            pltpu.VMEM((B, D), bf16),
            pltpu.VMEM((B + LIST, D), bf16),
            pltpu.SemaphoreType.DMA((B // CH,)),
            pltpu.SemaphoreType.DMA((2 * (B // CH) + 1,)),
        ],
        compiler_params=pltpu.CompilerParams(vmem_limit_bytes=GRANT),
        name="unit_rows",
    )(partners, pair_count, embeddings)


def halves_kernel(a_ref, b_ref, top_ref, low_ref, buf, sem):
    n = B // 2 // CH
    moves = []
    for i in range(2 * n):
        count = CH + LIST if i == 2 * n - 1 else CH
        src = a_ref.at[pl.ds(i * CH, count), :] if i < n else b_ref.at[pl.ds(i * CH, count), :]
        dst = top_ref.at[pl.ds(i * CH, count), :] if i < n else low_ref.at[pl.ds((i - n) * CH, count), :]
        held = buf.at[pl.ds(i * CH, count), :]
        moves.append((pltpu.make_async_copy(src, held, sem.at[2 * i]), pltpu.make_async_copy(held, dst, sem.at[2 * i + 1])))
    for load, _ in moves:
        load.start()
    for load, store in moves:
        load.wait()
        store.start()
    for _, store in moves:
        store.wait()


def halves(a, b):
    bf16, anywhere = jnp.bfloat16, pl.BlockSpec(memory_space=pl.ANY)
    return pl.pallas_call(
        halves_kernel,
        in_specs=[anywhere] * 2,
        out_specs=[anywhere] * 2,
        out_shape=[jax.ShapeDtypeStruct((B // 2, D), bf16), jax.ShapeDtypeStruct((B // 2 + LIST, D), bf16)],
        scratch_shapes=[pltpu.VMEM((B + LIST, D), bf16), pltpu.SemaphoreType.DMA((2 * B // CH,))],
        compiler_params=pltpu.CompilerParams(vmem_limit_bytes=GRANT),
        name="halves",
    )(a, b)


def lanes(value, op):
    return functools.reduce(op, [value[:, q * 128 : (q + 1) * 128] for q in range(value.shape[1] // 128)])


def rows8(value, op):
    return functools.reduce(op, [value[q * 8 : (q + 1) * 8, :] for q in range(value.shape[0] // 8)])


def fold(m, s, f, axis):
    top = jnp.max(m, axis, keepdims=True)
    plain = jnp.sum(f, axis, keepdims=True)
    top = jnp.maximum(top, jnp.where(plain > 0.0, 0.0, FLOOR))
    total = jnp.sum(s * jnp.exp2(m - top), axis, keepdims=True)
    total = total + plain * jnp.exp2(jnp.minimum(-top, 0.0))
    return jnp.maximum(top + jnp.log2(total), FLOOR)


def log2_add(a, b):
    top = jnp.maximum(a, b)
    return top + jnp.log2(jnp.exp2(a - top) + jnp.exp2(b - top))


def stage_kernel(plan, *refs):
    nl, nr, lefts, rights, widths, lists, wanted, nrow, ncol, own_first, last = plan
    row_prev, col_prev, refs = refs[: len(nrow)], refs[len(nrow) : len(nrow) + len(ncol)], refs[len(nrow) + len(ncol) :]
    blocks, refs = refs[: len(lefts) + len(rights)], refs[len(lefts) + len(rights) :]
    outs, refs = refs[:-SCRATCH], refs[-SCRATCH:]
    row_out, col_out = refs[-2:] if last else outs
    listed, flags, live, list_sem = refs[-6:-2]
    (lbuf, rbuf, sc, row_t, col_t, chk, row_f, row_m, row_s, col_f, col_m, col_s, waited, shifted, lsem, rsem) = refs[:-6]

    def copies(side, slot):
        pieces = lefts if side == 0 else rights
        base = 0 if side == 0 else len(lefts)
        buf, sem = (lbuf, lsem) if side == 0 else (rbuf, rsem)
        made = []
        for i, (s, src, dst, count) in enumerate(pieces):
            if s == slot:
                made.append(
                    pltpu.make_async_copy(
                        blocks[base + i].at[pl.ds(src, count), :], buf.at[slot, pl.ds(dst, count), :], sem.at[slot]
                    )
                )
        return made

    def used(flags):
        return functools.reduce(jnp.logical_or, [f > 0 for f in flags])

    me = lax.axis_index("dp")
    if own_first:
        live[0, 0] = 1
    else:
        fetched = [
            pltpu.make_async_copy(blocks[i].at[pl.ds(row, LIST), pl.ds(0, 128)], listed.at[q], list_sem.at[q])
            for q, (i, row) in enumerate(lists)
        ]
        for copy in fetched:
            copy.start()
        row_at = lax.broadcasted_iota(jnp.int32, (8, 128), 0)
        lane_at = lax.broadcasted_iota(jnp.int32, (8, 128), 1)
        found = jnp.zeros((8, 128), jnp.float32)
        for q in range(nl):
            fetched[q].wait()
            names = listed[q].astype(jnp.float32)[:8, :]
            for r in range(nr):
                if wanted[q][r]:
                    target = (me + RING * min(r, 2)).astype(jnp.float32)
                    hit = jnp.max(jnp.where(names == target, 1.0, 0.0), 1, keepdims=True)
                    found = jnp.where(jnp.logical_and(row_at == q, lane_at == r), hit, found)
        flags[...] = found.astype(jnp.int32)
        noted = pltpu.make_async_copy(flags, live, list_sem.at[nl])
        noted.start()
        noted.wait()

    need_l = [used([live[q, r] for r in range(nr)]) for q in range(nl)]
    need_r = [used([live[q, r] for q in range(nl)]) for r in range(nr)]

    def fetch(q):
        @pl.when(need_l[q])
        def _():
            for c in copies(0, q):
                c.start()

    fetch(0)
    for r in range(nr):
        waited[r] = 0

        @pl.when(need_r[r])
        def _(r=r):
            for c in copies(1, r):
                c.start()

    col_f[...] = jnp.zeros_like(col_f)
    col_s[...] = jnp.zeros_like(col_s)
    col_m[...] = jnp.full_like(col_m, FLOOR)

    def pair(q, r, width, diag):
        def dot(i):
            sc[i * CH : (i + 1) * CH, :width] = lax.dot_general(
                lbuf[q, i * CH : (i + 1) * CH, :],
                rbuf[r, :width, :],
                (((1,), (1,)), ((), ())),
                preferred_element_type=jnp.float32,
            )

        def sums(i):
            cols = jnp.zeros((8, width), jnp.float32)
            most = jnp.zeros((8, 128), jnp.float32)
            least = jnp.full((8, 128), MOST, jnp.float32)
            for g in range(CH // G):
                at = i * CH + g * G
                v = sc[at : at + G, :width]
                if diag:
                    r_at = lax.broadcasted_iota(jnp.int32, (G, width), 0) + at
                    c_at = lax.broadcasted_iota(jnp.int32, (G, width), 1)
                    eye = r_at == c_at
                    v = jnp.where(eye, MASKED, v)
                    sc[at : at + G, :width] = v
                e = jnp.exp2(v * GAIN)
                part = lanes(e, jnp.add)
                row_t[at : at + G, :] = part
                if not diag:
                    cols = cols + rows8(e, jnp.add)
                most = jnp.maximum(most, rows8(part, jnp.maximum))
                least = jnp.minimum(least, rows8(part, jnp.minimum))
            if not diag:
                if i:
                    cols = col_t[:, :width] + cols
                col_t[:, :width] = cols
                if i == B // CH - 1:
                    least = jnp.minimum(least, lanes(cols, jnp.minimum))
            if i:
                most, least = jnp.maximum(chk[0], most), jnp.minimum(chk[1], least)
            chk[0], chk[1] = most, least

        n = B // CH
        dot(0)
        for i in range(n):
            if i + 1 < n:
                dot(i + 1)
            sums(i)
        safe = jnp.logical_and(chk[0] <= MOST, chk[1] >= LEAST)
        plain = jnp.max(jnp.where(safe, 0.0, 1.0)) == 0.0

        @pl.when(plain)
        def _():
            row_f[...] += row_t[...]
            if not diag:
                col_f[r, :, :width] += col_t[:, :width]

        @pl.when(jnp.logical_not(plain))
        def _():
            @pl.when(shifted[0] == 0)
            def _():
                row_s[...] = jnp.zeros_like(row_s)
                row_m[...] = jnp.full_like(row_m, FLOOR)
                shifted[0] = 1

            def group(g, _):
                at = pl.multiple_of(g * G, G)
                w = sc[pl.ds(at, G), :width] * GAIN
                old = row_m[pl.ds(at, G), :]
                top = jnp.maximum(old, lanes(w, jnp.maximum))
                total = row_s[pl.ds(at, G), :] * jnp.exp2(old - top)
                for k in range(width // 128):
                    total = total + jnp.exp2(w[:, k * 128 : (k + 1) * 128] - top)
                row_m[pl.ds(at, G), :] = top
                row_s[pl.ds(at, G), :] = total
                if not diag:
                    old = col_m[r, :, :width]
                    top = jnp.maximum(old, rows8(w, jnp.maximum))
                    total = col_s[r, :, :width] * jnp.exp2(old - top)
                    for k in range(G // 8):
                        total = total + jnp.exp2(w[k * 8 : (k + 1) * 8, :] - top)
                    col_m[r, :, :width] = top
                    col_s[r, :, :width] = total
                return 0

            lax.fori_loop(0, B // G, group, 0)

    def arrive(r):
        @pl.when(waited[r] == 0)
        def _():
            for s in range(nr):

                @pl.when(r == s)
                def _(s=s):
                    for c in copies(1, s):
                        c.wait()

            waited[r] = 1

    def runs():
        start = 0
        for r in range(1, nr + 1):
            if r == nr or widths[r] != widths[start]:
                yield start, r, widths[start]
                start = r

    def left(q, _):
        needed = functools.reduce(jnp.logical_or, [live[q, r] > 0 for r in range(nr)])
        for s in range(1, nl):

            @pl.when(q + 1 == s)
            def _(s=s):
                fetch(s)

        row_out[pl.ds(q, 1), :] = jnp.full((1, B), FLOOR, jnp.float32)

        @pl.when(needed)
        def _():
            row_f[...] = jnp.zeros_like(row_f)
            shifted[0] = 0
            for s in range(nl):

                @pl.when(q == s)
                def _(s=s):
                    for c in copies(0, s):
                        c.wait()

            if own_first:

                @pl.when(q == 0)
                def _():
                    arrive(0)
                    pair(0, 0, B, True)

            for start, stop, width in runs():

                def step(r, _, width=width):
                    go = live[q, r] > 0
                    if own_first:
                        go = jnp.logical_and(go, q + r > 0)

                    @pl.when(go)
                    def _():
                        arrive(r)
                        pair(q, r, width, False)

                    return 0

                lax.fori_loop(start, stop, step, 0)

            @pl.when(shifted[0] == 0)
            def _():
                row_out[pl.ds(q, 1), :] = jnp.log2(jnp.sum(row_f[...].T, 0, keepdims=True))

            @pl.when(shifted[0] > 0)
            def _():
                row_out[pl.ds(q, 1), :] = fold(row_m[...].T, row_s[...].T, row_f[...].T, 0)

        return 0

    lax.fori_loop(0, nl, left, 0)
    for r in range(nr):
        col_out[r : r + 1, :] = jnp.full((1, B), FLOOR, jnp.float32)

        @pl.when(need_r[r])
        def _(r=r):
            col_out[r : r + 1, :] = fold(col_m[r], col_s[r], col_f[r], 0)

    for out, prevs in ((row_out, () if last else row_prev), (col_out, col_prev)):
        at = 0
        for prev in prevs:
            to = at + prev.shape[0]
            out[at:to, :] = log2_add(out[at:to, :], prev[...])
            at = to

    if last:
        ring_out, next_out, after_out = outs
        chip, core = me % RING // 2, me % 2
        for q in range(RING):
            at = (chip + PLACES[q][0]) % 4 * 2 + (core + PLACES[q][1]) % 2
            row = row_out[0:1, :] if q == RING - 1 else row_prev[0][q : q + 1, :]
            ring_out[at] = row if q else log2_add(row, col_out[0:1, :])
        next_out[...] = col_out[1:2, :]
        after_out[:, : B // 2] = col_out[3:4, : B // 2]
        after_out[:, B // 2 :] = col_out[2:3, : B // 2]


def stage(name, wanted, lefts, rights, row_prev=(), col_prev=(), own_first=False, last=False):
    nl, nr = len(lefts), len(rights)
    flat, tables = [], []
    for side in (lefts, rights):
        table = []
        for slot, pieces in enumerate(side):
            for array, src, dst, count in pieces:
                flat.append(array)
                table.append((slot, src, dst, count))
        tables.append(tuple(table))
    widths = tuple(sum(piece[3] for piece in pieces) for pieces in rights)
    nrow, ncol = tuple(p.shape[0] for p in row_prev), tuple(p.shape[0] for p in col_prev)
    lists, at = [], 0
    for pieces in lefts:
        at += len(pieces)
        lists.append((at - 1, pieces[-1][3]))
    plan = (nl, nr, tables[0], tables[1], widths, lists, wanted, nrow, ncol, own_first, last)
    cost = 2 * B * B * D * 4 if own_first else B
    f32 = jnp.float32
    shapes = [(RING, 1, B), (1, B), (1, B)] if last else [(nl, B), (nr, B)]
    shapes = [jax.ShapeDtypeStruct(shape, f32) for shape in shapes]
    return pl.pallas_call(
        functools.partial(stage_kernel, plan),
        out_shape=shapes,
        in_specs=[pl.BlockSpec(memory_space=pltpu.VMEM)] * (len(nrow) + len(ncol))
        + [pl.BlockSpec(memory_space=pl.ANY)] * len(flat),
        out_specs=[pl.BlockSpec(memory_space=pltpu.VMEM)] * len(shapes),
        scratch_shapes=[
            pltpu.VMEM((nl, B, D), jnp.bfloat16),
            pltpu.VMEM((nr, B, D), jnp.bfloat16),
            pltpu.VMEM((B, B), f32),
            pltpu.VMEM((B, 128), f32),
            pltpu.VMEM((8, B), f32),
            pltpu.VMEM((2, 8, 128), f32),
            pltpu.VMEM((B, 128), f32),
            pltpu.VMEM((B, 128), f32),
            pltpu.VMEM((B, 128), f32),
            pltpu.VMEM((nr, 8, B), f32),
            pltpu.VMEM((nr, 8, B), f32),
            pltpu.VMEM((nr, 8, B), f32),
            pltpu.SMEM((nr,), jnp.int32),
            pltpu.SMEM((1,), jnp.int32),
            pltpu.SemaphoreType.DMA((nl,)),
            pltpu.SemaphoreType.DMA((nr,)),
            pltpu.VMEM((nl, LIST, 128), jnp.bfloat16),
            pltpu.VMEM((8, 128), jnp.int32),
            pltpu.SMEM((8, 128), jnp.int32),
            pltpu.SemaphoreType.DMA((nl + 1,)),
            pltpu.VMEM((nl, B), f32),
            pltpu.VMEM((nr, B), f32),
        ],
        compiler_params=pltpu.CompilerParams(vmem_limit_bytes=GRANT),
        cost_estimate=pl.CostEstimate(
            flops=cost, bytes_accessed=B, transcendentals=0
        ),
        name=name,
    )(*row_prev, *col_prev, *flat)


def last_kernel(row_ref, ring_ref, *refs):
    parts, o_ref = refs[:-1], refs[-1]
    row = row_ref[0]
    got = [ring_ref[k] for k in range(RING)]
    for k, part in enumerate(parts):
        got.append(jnp.where(row > k, part[...], FLOOR))
    got = jnp.concatenate(got, 0)
    best = jnp.max(got, 0, keepdims=True)
    total = jnp.sum(jnp.exp2(got - best), 0, keepdims=True)
    o_ref[...] = (best + jnp.log2(total)) * (LN2 / SCALE)


def body(embeddings, partners, pair_count):
    unit, top, low = normalize(embeddings, partners, pair_count)
    me = lax.axis_index("dp")
    swap = along(0, 1)
    together = lax.optimization_barrier

    over, on = [], []
    for d in range(2 * RING, COUNT):
        z, y = d // 32, (d // RING) % 4
        relay = (z - (y < 2)) * 32 + (y + 1) % 4 * RING + d % RING
        over.append((d, relay))
        on.append((relay, d - 2 * RING))

    def whole(array):
        return [(array, 0, 0, B)]

    a = send(unit, around(1))
    b = send(unit, around(-1))
    relayed = send(low, over)
    c = send(unit, along(-RING))
    row_0, _ = stage("own", ((1,),), [whole(unit)], [whole(unit)], own_first=True)
    relayed, row_0, late = together((relayed, row_0, unit))
    d_low = send(relayed, on)
    sib = send(late, swap)
    a, b, c, d_low, sib = together((a, b, c, d_low, sib))

    a_top, b_low = halves(a, b)
    f_top = send(a_top, around(1))
    f_low = send(b_low, around(-1))
    a, b, top, a_top = together((a, b, top, a_top))
    d_top = send(top, along(-2 * RING))
    a_sib = send(a, swap)
    b_sib = send(b, swap)

    rights = [whole(unit), whole(c), [(d_low, 0, 0, H)]]
    lefts = [whole(unit), whole(sib), whole(a), whole(b)]
    row_1, col_1 = stage("near", ((0, 1, 1),) + ((1, 1, 1),) * 3, lefts, rights, [row_0], [])
    a_sib, b_sib, row_1 = together((a_sib, b_sib, row_1))
    row_2, col_2 = stage("mid", ((1, 1, 1),) * 2, [whole(a_sib), whole(b_sib)], rights, [], [col_1])
    f_top, f_low, d_top, row_2 = together((f_top, f_low, d_top, row_2))
    f_top_sib = send(f_top, swap)
    f_low_sib = send(f_low, swap)

    rights = rights + [[(d_top, 0, 0, H)]]
    lefts = lefts + [whole(a_sib), whole(b_sib), [(f_top, 0, 0, H), (f_low, 0, H, H)]]
    wanted = ((0, 0, 0, 1),) * 6 + ((1, 1, 1, 1),)
    row_3, col_3 = stage("far", wanted, lefts, rights, [row_1, row_2], [col_2])
    f_low_sib, f_top_sib, row_3 = together((f_low_sib, f_top_sib, row_3))
    lefts = [[(f_top_sib, 0, 0, H), (f_low_sib, 0, H, H)]]
    ring_part, next_part, after_part = stage("last", ((1, 1, 1, 1),), lefts, rights, [row_3], [col_3], last=True)

    next_got = send(next_part, along(RING))
    after_got = send(after_part, along(2 * RING))
    groups = [[r * RING + k for k in range(RING)] for r in range(COUNT // RING)]
    ring_got = lax.all_to_all(ring_part, "dp", 0, 0, axis_index_groups=groups, tiled=True)
    out = pl.pallas_call(
        last_kernel,
        in_specs=[pl.BlockSpec(memory_space=pltpu.SMEM)] + [pl.BlockSpec(memory_space=pltpu.VMEM)] * 3,
        out_shape=jax.ShapeDtypeStruct((1, B), jnp.float32),
        name="last_sum",
    )((me // RING)[None].astype(jnp.int32), ring_got, next_got, after_got)
    return out.reshape(B)


def solution(mesh):
    placed = (P("dp", None), P("dp", None), P("dp"))
    return jax.shard_map(body, mesh=mesh, in_specs=placed, out_specs=P("dp"), check_vma=False)
```

profile of v0, /device:TPU:66, one launch (start us, length us, event | category | flops | bytes accessed | tf_op | source)
XLA Modules:
  0.0 140.0 jit_solution(7981286913081545950)
XLA Ops:
  0.7 4.1 %unit_rows.1 = (bf16[1040,1024]{1,0:T(8,128)(2,1)}, bf16[512,1024]{1,0:T(8,128)(2,1)}, bf16[512,1024]{1,0:T(8,128)(2,1)}) custom-call(s32[1,13]{1,0:T(1,128)} %list_ref.1, s32[1]{0:T(128)S(6)} %copy.4.count_ref, bf16[1024,1024]{1,0:T(8,128)(2,1)} %x_ref.1), custom_call_target="tpu_custom_call" | custom-call | tf_op jit(solution)/shard_map/unit_rows/pallas_call | solution.py:82
  4.8 3.0 %collective-permute-start.3 = (bf16[512,1024]{1,0:T(8,128)(2,1)}, bf16[512,1024]{1,0:T(8,128)(2,1)}, u32[]{:S(2)}, u32[]{:S(2)}) collective-permute-start(bf16[512,1024]{1,0:T(8,128)(2,1)} %get-tuple-element.42), channel_id=1, source_target_pairs={{16,24},{17,25},{18,26},{19,27},{20,28},{21,29},{22,30},{23,31},{2... | collective-permute-start | bytes 3145736 | tf_op jit(solution)/shard_map/ppermute | solution.py:45
  7.8 3.6 %collective-permute-start.2 = (bf16[1040,1024]{1,0:T(8,128)(2,1)}, bf16[1040,1024]{1,0:T(8,128)(2,1)}, u32[]{:S(2)}, u32[]{:S(2)}) collective-permute-start(bf16[1040,1024]{1,0:T(8,128)(2,1)} %get-tuple-element.45.refs_0_.refs_1_.refs_5_.refs_3_.refs_11_.refs_4_), channel_id=1, source_target_pairs={{8,0},{9,1},{10,2},{11,3},{12,4},{13,5},{14,6},{15,7},{16,8},{17,9... | collective-permute-start | bytes 6389768 | tf_op jit(solution)/shard_map/ppermute | solution.py:45
  11.4 0.6 collective-permute-start.1
  12.0 1.5 %collective-permute-start = (bf16[1040,1024]{1,0:T(8,128)(2,1)}, bf16[1040,1024]{1,0:T(8,128)(2,1)}, u32[]{:S(2)}, u32[]{:S(2)}) collective-permute-start(bf16[1040,1024]{1,0:T(8,128)(2,1)} %get-tuple-element.45.refs_0_.refs_1_.refs_5_.refs_3_.refs_11_.refs_4_), channel_id=1, source_target_pairs={{0,2},{1,3},{2,4},{3,5},{4,6},{5,7},{6,0},{7,1},{8,10},{9,11},{10,... | collective-permute-start | bytes 6389768 | tf_op jit(solution)/shard_map/ppermute | solution.py:45
  13.5 7.3 %own.1 = (f32[1,1024]{1,0:T(1,128)}, f32[1,1024]{1,0:T(1,128)}) custom-call(bf16[1040,1024]{1,0:T(8,128)(2,1)} %get-tuple-element.45.refs_0_.refs_1_.refs_5_.refs_3_.refs_11_.refs_4_, bf16[1040,1024]{1,0:T(8,128)(2,1)} %get-tuple-element.45.refs_0_.refs_1_.refs_5_.refs_3_.refs_11_.refs_4_), custom_call_target="tpu_custom_call" | custom-call | flops 8589934592 | bytes 1024 | tf_op jit(solution)/shard_map/own/pallas_call | solution.py:434
  20.8 12.3 %collective-permute-done.3 = bf16[512,1024]{1,0:T(8,128)(2,1)} collective-permute-done((bf16[512,1024]{1,0:T(8,128)(2,1)}, bf16[512,1024]{1,0:T(8,128)(2,1)}, u32[]{:S(2)}, u32[]{:S(2)}) %collective-permute-start.3) | collective-permute-done | bytes 1048608 | tf_op jit(solution)/shard_map/ppermute | solution.py:45
  33.2 0.0 collective-permute-start.5
  33.2 3.1 %collective-permute-start.4 = (bf16[512,1024]{1,0:T(8,128)(2,1)}, bf16[512,1024]{1,0:T(8,128)(2,1)}, u32[]{:S(2)}, u32[]{:S(2)}) collective-permute-start(bf16[512,1024]{1,0:T(8,128)(2,1)} %collective-permute-done.3), channel_id=1, source_target_pairs={{24,0},{25,1},{26,2},{27,3},{28,4},{29,5},{30,6},{31,7},{0,8},{1,9... | collective-permute-start | bytes 3145736 | tf_op jit(solution)/shard_map/ppermute | solution.py:45
  36.3 25.9 %collective-permute-done.4.refs_7_.refs_5_.refs_13_.refs_6_ = bf16[512,1024]{1,0:T(8,128)(2,1)} collective-permute-done((bf16[512,1024]{1,0:T(8,128)(2,1)}, bf16[512,1024]{1,0:T(8,128)(2,1)}, u32[]{:S(2)}, u32[]{:S(2)}) %collective-permute-start.4) | collective-permute-done | bytes 1048608 | tf_op jit(solution)/shard_map/ppermute | solution.py:45
  62.2 0.0 collective-permute-done.2.refs_6_.refs_4_.refs_12_.refs_5_
  62.2 0.0 collective-permute-done.1.b_ref.refs_4_.refs_6_
  62.2 0.0 collective-permute-done.a_ref.refs_3_.refs_5_
  62.2 0.0 collective-permute-done.5.refs_2_.refs_4_
  62.2 2.5 %halves.1 = (bf16[512,1024]{1,0:T(8,128)(2,1)}, bf16[528,1024]{1,0:T(8,128)(2,1)}) custom-call(bf16[1040,1024]{1,0:T(8,128)(2,1)} %collective-permute-done.a_ref.refs_3_.refs_5_, bf16[1040,1024]{1,0:T(8,128)(2,1)} %collective-permute-done.1.b_ref.refs_4_.refs_6_), custom_call_target="tpu_custom_call" | custom-call | tf_op jit(solution)/shard_map/halves/pallas_call | solution.py:122
  64.7 0.1 collective-permute-start.9
  64.8 0.5 collective-permute-start.10
  65.3 1.4 %collective-permute-start.7 = (bf16[528,1024]{1,0:T(8,128)(2,1)}, bf16[528,1024]{1,0:T(8,128)(2,1)}, u32[]{:S(2)}, u32[]{:S(2)}) collective-permute-start(bf16[528,1024]{1,0:T(8,128)(2,1)} %get-tuple-element.49), channel_id=1, source_target_pairs={{0,6},{1,7},{2,0},{3,1},{4,2},{5,3},{6,4},{7,5},{8,14},{9,15},{10,... | collective-permute-start | bytes 3244040 | tf_op jit(solution)/shard_map/ppermute | solution.py:45
  66.7 3.4 %collective-permute-start.8 = (bf16[512,1024]{1,0:T(8,128)(2,1)}, bf16[512,1024]{1,0:T(8,128)(2,1)}, u32[]{:S(2)}, u32[]{:S(2)}) collective-permute-start(bf16[512,1024]{1,0:T(8,128)(2,1)} %get-tuple-element.51), channel_id=1, source_target_pairs={{16,0},{17,1},{18,2},{19,3},{20,4},{21,5},{22,6},{23,7},{24,8},{25... | collective-permute-start | bytes 3145736 | tf_op jit(solution)/shard_map/ppermute | solution.py:45
  70.1 0.4 collective-permute-start.6
  70.4 13.8 %near.1 = (f32[4,1024]{1,0:T(4,128)}, f32[3,1024]{1,0:T(4,128)}) custom-call(f32[1,1024]{1,0:T(1,128)} %get-tuple-element.52.refs_0_, bf16[1040,1024]{1,0:T(8,128)(2,1)} %get-tuple-element.45.refs_0_.refs_1_.refs_5_.refs_3_.refs_11_.refs_4_, bf16[1040,1024]{1,0:T(8,128)(2,1)} %collective-permute-done.5.refs_2_.refs_4_, ...), custom_call_target="tpu_custom_call" | custom-call | flops 1024 | bytes 1024 | tf_op jit(solution)/shard_map/near/pallas_call | solution.py:434
  84.3 0.0 collective-permute-done.9.refs_1_.refs_7_
  84.3 0.0 collective-permute-done.10.refs_2_.refs_8_
  84.3 2.9 %mid.1 = (f32[2,1024]{1,0:T(2,128)}, f32[3,1024]{1,0:T(4,128)}) custom-call(f32[3,1024]{1,0:T(4,128)} %get-tuple-element.58.refs_0_, bf16[1040,1024]{1,0:T(8,128)(2,1)} %collective-permute-done.9.refs_1_.refs_7_, bf16[1040,1024]{1,0:T(8,128)(2,1)} %collective-permute-done.10.refs_2_.refs_8_, ...), custom_call_target="tpu_custom_call" | custom-call | flops 1024 | bytes 1024 | tf_op jit(solution)/shard_map/mid/pallas_call | solution.py:434
  87.2 8.1 %collective-permute-done.8.refs_14_.refs_7_ = bf16[512,1024]{1,0:T(8,128)(2,1)} collective-permute-done((bf16[512,1024]{1,0:T(8,128)(2,1)}, bf16[512,1024]{1,0:T(8,128)(2,1)}, u32[]{:S(2)}, u32[]{:S(2)}) %collective-permute-start.8) | collective-permute-done | bytes 1048608 | tf_op jit(solution)/shard_map/ppermute | solution.py:45
  95.3 0.0 collective-permute-done.6.refs_9_
  95.3 0.0 collective-permute-done.7.refs_10_
  95.3 0.0 collective-permute-start.11
  95.3 0.5 collective-permute-start.12
  95.8 15.7 %far.1 = (f32[7,1024]{1,0:T(8,128)}, f32[4,1024]{1,0:T(4,128)}) custom-call(f32[4,1024]{1,0:T(4,128)} %get-tuple-element.65.refs_0_, f32[2,1024]{1,0:T(2,128)} %get-tuple-element.66.refs_1_, f32[3,1024]{1,0:T(4,128)} %get-tuple-element.67.refs_2_, bf16[1040,1024]{1,0:T(8,128)(2,1)} %get-tuple-element.45.refs_0_.refs_1_.refs_5_.refs_3_.refs_11_.refs_4_, ...), custom_call_target="tpu_custom_call" | custom-call | flops 1024 | bytes 1024 | tf_op jit(solution)/shard_map/far/pallas_call | solution.py:434
  111.5 0.0 collective-permute-done.12.refs_2_
  111.5 0.0 collective-permute-done.11.refs_3_
  111.5 2.9 %last.1 = (f32[8,1,1024]{2,1,0:T(1,128)}, f32[1,1024]{1,0:T(1,128)}, f32[1,1024]{1,0:T(1,128)}) custom-call(f32[7,1024]{1,0:T(8,128)} %get-tuple-element.70.refs_0_, f32[4,1024]{1,0:T(4,128)} %get-tuple-element.71.refs_1_, bf16[512,1024]{1,0:T(8,128)(2,1)} %collective-permute-done.12.refs_2_, bf16[528,1024]{1,0:T(8,128)(2,1)} %collective-permute-done.11.refs_3_, ...), custom_call_target="tpu_custom_call" | custom-call | flops 1024 | bytes 1024 | tf_op jit(solution)/shard_map/last/pallas_call | solution.py:434
  114.4 7.2 %all-to-all-start = ((f32[8,1,1024]{2,1,0:T(1,128)}), f32[8,1,1024]{2,1,0:T(1,128)S(1)}, u32[]{:S(2)}, u32[]{:S(2)}) async-start(f32[8,1,1024]{2,1,0:T(1,128)} %get-tuple-element.74), calls=%async_computation | async-start | bytes 65536 | tf_op jit(solution)/shard_map/all_to_all | solution.py:538
  121.6 1.9 %collective-permute-start.13 = (f32[1,1024]{1,0:T(1,128)}, f32[1,1024]{1,0:T(1,128)S(1)}, u32[]{:S(2)}, u32[]{:S(2)}) collective-permute-start(f32[1,1024]{1,0:T(1,128)} %get-tuple-element.75), channel_id=1, source_target_pairs={{0,8},{1,9},{2,10},{3,11},{4,12},{5,13},{6,14},{7,15},{8,16},{9,17... | collective-permute-start | bytes 12296 | tf_op jit(solution)/shard_map/ppermute | solution.py:45
  123.6 12.8 %collective-permute-start.14 = (f32[1,1024]{1,0:T(1,128)}, f32[1,1024]{1,0:T(1,128)S(1)}, u32[]{:S(2)}, u32[]{:S(2)}) collective-permute-start(f32[1,1024]{1,0:T(1,128)} %get-tuple-element.76), channel_id=1, source_target_pairs={{0,16},{1,17},{2,18},{3,19},{4,20},{5,21},{6,22},{7,23},{8,24},{9,... | collective-permute-start | bytes 12296 | tf_op jit(solution)/shard_map/ppermute | solution.py:45
  136.4 0.0 collective-permute-done.13.refs_0_
  136.4 0.0 copy-start.1
  136.4 1.5 %collective-permute-done.14.refs_1_ = f32[1,1024]{1,0:T(1,128)S(1)} collective-permute-done((f32[1,1024]{1,0:T(1,128)}, f32[1,1024]{1,0:T(1,128)S(1)}, u32[]{:S(2)}, u32[]{:S(2)}) %collective-permute-start.14) | collective-permute-done | bytes 4128 | tf_op jit(solution)/shard_map/ppermute | solution.py:45
  137.9 0.0 copy-start.2
  137.9 0.0 all-to-all-done.ring_ref
  137.9 0.0 copy-start
  137.9 0.0 copy-done.1
  137.9 0.6 copy-done.2
  138.5 0.0 copy-done
  138.5 1.4 %last_sum.1 = f32[1,1024]{1,0:T(1,128)} custom-call(s32[1]{0:T(128)} %bitcast.row_ref, f32[8,1,1024]{2,1,0:T(1,128)} %copy-done, f32[1,1024]{1,0:T(1,128)} %copy-done.1, f32[1,1024]{1,0:T(1,128)} %copy-done.2), custom_call_target="tpu_custom_call" | custom-call | tf_op jit(solution)/shard_map/last_sum/pallas_call | solution.py:539
Async XLA Ops:
  4.8 28.4 %collective-permute-start.3 = (bf16[512,1024]{1,0:T(8,128)(2,1)}, bf16[512,1024]{1,0:T(8,128)(2,1)}, u32[]{:S(2)}, u32[]{:S(2)}) collective-permute-start(bf16[512,1024]{1,0:T(8,128)(2,1)} %get-tuple-element.42), channel_id=1, source_target_pairs={{16,24},{17,25},{18,26},{19,27},{20,28},{21,29},{22,30},{23,31},{2... | collective-permute-start | bytes 3145736 | tf_op jit(solution)/shard_map/ppermute | solution.py:45
  7.8 54.3 %collective-permute-start.2 = (bf16[1040,1024]{1,0:T(8,128)(2,1)}, bf16[1040,1024]{1,0:T(8,128)(2,1)}, u32[]{:S(2)}, u32[]{:S(2)}) collective-permute-start(bf16[1040,1024]{1,0:T(8,128)(2,1)} %get-tuple-element.45.refs_0_.refs_1_.refs_5_.refs_3_.refs_11_.refs_4_), channel_id=1, source_target_pairs={{8,0},{9,1},{10,2},{11,3},{12,4},{13,5},{14,6},{15,7},{16,8},{17,9... | collective-permute-start | bytes 6389768 | tf_op jit(solution)/shard_map/ppermute | solution.py:45
  11.4 50.8 %collective-permute-start.1 = (bf16[1040,1024]{1,0:T(8,128)(2,1)}, bf16[1040,1024]{1,0:T(8,128)(2,1)}, u32[]{:S(2)}, u32[]{:S(2)}) collective-permute-start(bf16[1040,1024]{1,0:T(8,128)(2,1)} %get-tuple-element.45.refs_0_.refs_1_.refs_5_.refs_3_.refs_11_.refs_4_), channel_id=1, source_target_pairs={{0,6},{1,7},{2,0},{3,1},{4,2},{5,3},{6,4},{7,5},{8,14},{9,15},{10,... | collective-permute-start | bytes 6389768 | tf_op jit(solution)/shard_map/ppermute | solution.py:45
  12.0 50.2 %collective-permute-start = (bf16[1040,1024]{1,0:T(8,128)(2,1)}, bf16[1040,1024]{1,0:T(8,128)(2,1)}, u32[]{:S(2)}, u32[]{:S(2)}) collective-permute-start(bf16[1040,1024]{1,0:T(8,128)(2,1)} %get-tuple-element.45.refs_0_.refs_1_.refs_5_.refs_3_.refs_11_.refs_4_), channel_id=1, source_target_pairs={{0,2},{1,3},{2,4},{3,5},{4,6},{5,7},{6,0},{7,1},{8,10},{9,11},{10,... | collective-permute-start | bytes 6389768 | tf_op jit(solution)/shard_map/ppermute | solution.py:45
  33.2 29.0 %collective-permute-start.5 = (bf16[1040,1024]{1,0:T(8,128)(2,1)}, bf16[1040,1024]{1,0:T(8,128)(2,1)}, u32[]{:S(2)}, u32[]{:S(2)}) collective-permute-start(bf16[1040,1024]{1,0:T(8,128)(2,1)} %get-tuple-element.45.refs_0_.refs_1_.refs_5_.refs_3_.refs_11_.refs_4_), channel_id=1, source_target_pairs={{0,1},{1,0},{2,3},{3,2},{4,5},{5,4},{6,7},{7,6},{8,9},{9,8},{10,11... | collective-permute-start | bytes 6389768 | tf_op jit(solution)/shard_map/ppermute | solution.py:45
  33.2 29.0 %collective-permute-start.4 = (bf16[512,1024]{1,0:T(8,128)(2,1)}, bf16[512,1024]{1,0:T(8,128)(2,1)}, u32[]{:S(2)}, u32[]{:S(2)}) collective-permute-start(bf16[512,1024]{1,0:T(8,128)(2,1)} %collective-permute-done.3), channel_id=1, source_target_pairs={{24,0},{25,1},{26,2},{27,3},{28,4},{29,5},{30,6},{31,7},{0,8},{1,9... | collective-permute-start | bytes 3145736 | tf_op jit(solution)/shard_map/ppermute | solution.py:45
  64.7 19.6 %collective-permute-start.9 = (bf16[1040,1024]{1,0:T(8,128)(2,1)}, bf16[1040,1024]{1,0:T(8,128)(2,1)}, u32[]{:S(2)}, u32[]{:S(2)}) collective-permute-start(bf16[1040,1024]{1,0:T(8,128)(2,1)} %collective-permute-done.a_ref.refs_3_.refs_5_), channel_id=1, source_target_pairs={{0,1},{1,0},{2,3},{3,2},{4,5},{5,4},{6,7},{7,6},{8,9},{9,8},{10,11... | collective-permute-start | bytes 6389768 | tf_op jit(solution)/shard_map/ppermute | solution.py:45
  64.8 19.5 %collective-permute-start.10 = (bf16[1040,1024]{1,0:T(8,128)(2,1)}, bf16[1040,1024]{1,0:T(8,128)(2,1)}, u32[]{:S(2)}, u32[]{:S(2)}) collective-permute-start(bf16[1040,1024]{1,0:T(8,128)(2,1)} %collective-permute-done.1.b_ref.refs_4_.refs_6_), channel_id=1, source_target_pairs={{0,1},{1,0},{2,3},{3,2},{4,5},{5,4},{6,7},{7,6},{8,9},{9,8},{10,11... | collective-permute-start | bytes 6389768 | tf_op jit(solution)/shard_map/ppermute | solution.py:45
  65.3 30.0 %collective-permute-start.7 = (bf16[528,1024]{1,0:T(8,128)(2,1)}, bf16[528,1024]{1,0:T(8,128)(2,1)}, u32[]{:S(2)}, u32[]{:S(2)}) collective-permute-start(bf16[528,1024]{1,0:T(8,128)(2,1)} %get-tuple-element.49), channel_id=1, source_target_pairs={{0,6},{1,7},{2,0},{3,1},{4,2},{5,3},{6,4},{7,5},{8,14},{9,15},{10,... | collective-permute-start | bytes 3244040 | tf_op jit(solution)/shard_map/ppermute | solution.py:45
  66.7 28.6 %collective-permute-start.8 = (bf16[512,1024]{1,0:T(8,128)(2,1)}, bf16[512,1024]{1,0:T(8,128)(2,1)}, u32[]{:S(2)}, u32[]{:S(2)}) collective-permute-start(bf16[512,1024]{1,0:T(8,128)(2,1)} %get-tuple-element.51), channel_id=1, source_target_pairs={{16,0},{17,1},{18,2},{19,3},{20,4},{21,5},{22,6},{23,7},{24,8},{25... | collective-permute-start | bytes 3145736 | tf_op jit(solution)/shard_map/ppermute | solution.py:45
  70.1 25.2 %collective-permute-start.6 = (bf16[512,1024]{1,0:T(8,128)(2,1)}, bf16[512,1024]{1,0:T(8,128)(2,1)}, u32[]{:S(2)}, u32[]{:S(2)}) collective-permute-start(bf16[512,1024]{1,0:T(8,128)(2,1)} %get-tuple-element.48), channel_id=1, source_target_pairs={{0,2},{1,3},{2,4},{3,5},{4,6},{5,7},{6,0},{7,1},{8,10},{9,11},{10,... | collective-permute-start | bytes 3145736 | tf_op jit(solution)/shard_map/ppermute | solution.py:45
  95.3 16.2 %collective-permute-start.11 = (bf16[528,1024]{1,0:T(8,128)(2,1)}, bf16[528,1024]{1,0:T(8,128)(2,1)}, u32[]{:S(2)}, u32[]{:S(2)}) collective-permute-start(bf16[528,1024]{1,0:T(8,128)(2,1)} %collective-permute-done.7.refs_10_), channel_id=1, source_target_pairs={{0,1},{1,0},{2,3},{3,2},{4,5},{5,4},{6,7},{7,6},{8,9},{9,8},{10,11... | collective-permute-start | bytes 3244040 | tf_op jit(solution)/shard_map/ppermute | solution.py:45
  95.3 16.2 %collective-permute-start.12 = (bf16[512,1024]{1,0:T(8,128)(2,1)}, bf16[512,1024]{1,0:T(8,128)(2,1)}, u32[]{:S(2)}, u32[]{:S(2)}) collective-permute-start(bf16[512,1024]{1,0:T(8,128)(2,1)} %collective-permute-done.6.refs_9_), channel_id=1, source_target_pairs={{0,1},{1,0},{2,3},{3,2},{4,5},{5,4},{6,7},{7,6},{8,9},{9,8},{10,11... | collective-permute-start | bytes 3145736 | tf_op jit(solution)/shard_map/ppermute | solution.py:45
  114.4 23.5 %all-to-all-start = ((f32[8,1,1024]{2,1,0:T(1,128)}), f32[8,1,1024]{2,1,0:T(1,128)S(1)}, u32[]{:S(2)}, u32[]{:S(2)}) async-start(f32[8,1,1024]{2,1,0:T(1,128)} %get-tuple-element.74), calls=%async_computation | async-start | bytes 65536 | tf_op jit(solution)/shard_map/all_to_all | solution.py:538
  121.6 14.8 %collective-permute-start.13 = (f32[1,1024]{1,0:T(1,128)}, f32[1,1024]{1,0:T(1,128)S(1)}, u32[]{:S(2)}, u32[]{:S(2)}) collective-permute-start(f32[1,1024]{1,0:T(1,128)} %get-tuple-element.75), channel_id=1, source_target_pairs={{0,8},{1,9},{2,10},{3,11},{4,12},{5,13},{6,14},{7,15},{8,16},{9,17... | collective-permute-start | bytes 12296 | tf_op jit(solution)/shard_map/ppermute | solution.py:45
  123.6 14.4 %collective-permute-start.14 = (f32[1,1024]{1,0:T(1,128)}, f32[1,1024]{1,0:T(1,128)S(1)}, u32[]{:S(2)}, u32[]{:S(2)}) collective-permute-start(f32[1,1024]{1,0:T(1,128)} %get-tuple-element.76), channel_id=1, source_target_pairs={{0,16},{1,17},{2,18},{3,19},{4,20},{5,21},{6,22},{7,23},{8,24},{9,... | collective-permute-start | bytes 12296 | tf_op jit(solution)/shard_map/ppermute | solution.py:45
  136.4 1.5 %copy-start.1 = (f32[1,1024]{1,0:T(1,128)}, f32[1,1024]{1,0:T(1,128)S(1)}, u32[]{:S(2)}) copy-start(f32[1,1024]{1,0:T(1,128)S(1)} %collective-permute-done.13.refs_0_) | copy-start | bytes 12292
  137.9 0.6 copy-start.2
  137.9 0.6 copy-start
where the time goes:
time: 139 us; the launch traced here: 140 us
  Pallas kernels  50.7 us (36%)
  waiting for transfers between devices  47.8 us (34%)
  starting transfers between devices  40 us (29%)
    ppermute x15, waiting for transfers between devices, send(): return lax.ppermute(value, 'dp', moves)  47.8 us
    pallas_call x5, Pallas kernels, stage(): pl.pallas_call(functools.partial(stage_kernel, plan), out_shape=shapes, i...  42.6 us
    ppermute x15, starting transfers between devices, send(): return lax.ppermute(value, 'dp', moves)  32.8 us
    all_to_all x1, starting transfers between devices, body(): lax.all_to_all(ring_part, 'dp', 0, 0, axis_index_groups=groups, tiled=True)  7.25 us
    pallas_call x1, Pallas kernels, normalize(): pl.pallas_call(unit_kernel, in_specs=[smem, smem, anywhere], out_specs=[a...  4.12 us
  transfers between devices with their start and end apart: 16, of which 4 were waited for; matrix products, arithmetic and copies ran while one was open for 0% of the time, Pallas kernels for 28%

commit v1 on v0

--- a/solution.py
+++ b/solution.py
@@ -469,9 +469,9 @@
     )(*row_prev, *col_prev, *flat)
 
 
-def last_kernel(row_ref, ring_ref, *refs):
+def last_kernel(ring_ref, *refs):
     parts, o_ref = refs[:-1], refs[-1]
-    row = row_ref[0]
+    row = lax.axis_index("dp") // RING
     got = [ring_ref[k] for k in range(RING)]
     for k, part in enumerate(parts):
         got.append(jnp.where(row > k, part[...], FLOOR))
@@ -483,7 +483,6 @@
 
 def body(embeddings, partners, pair_count):
     unit, top, low = normalize(embeddings, partners, pair_count)
-    me = lax.axis_index("dp")
     swap = along(0, 1)
     together = lax.optimization_barrier
 
@@ -505,12 +504,13 @@
     relayed, row_0, late = together((relayed, row_0, unit))
     d_low = send(relayed, on)
     sib = send(late, swap)
-    a, b, c, d_low, sib = together((a, b, c, d_low, sib))
+    a, b = together((a, b))
 
     a_top, b_low = halves(a, b)
     f_top = send(a_top, around(1))
     f_low = send(b_low, around(-1))
-    a, b, top, a_top = together((a, b, top, a_top))
+    c, d_low, sib = together((c, d_low, sib))
+    a, b, top, a_top, c = together((a, b, top, a_top, c))
     d_top = send(top, along(-2 * RING))
     a_sib = send(a, swap)
     b_sib = send(b, swap)
@@ -538,10 +538,9 @@
     ring_got = lax.all_to_all(ring_part, "dp", 0, 0, axis_index_groups=groups, tiled=True)
     out = pl.pallas_call(
         last_kernel,
-        in_specs=[pl.BlockSpec(memory_space=pltpu.SMEM)] + [pl.BlockSpec(memory_space=pltpu.VMEM)] * 3,
         out_shape=jax.ShapeDtypeStruct((1, B), jnp.float32),
         name="last_sum",
-    )((me // RING)[None].astype(jnp.int32), ring_got, next_got, after_got)
+    )(ring_got, next_got, after_got)
     return out.reshape(B)
 
 

time: 139 us -> 140 us (level)
  the two profiles are of different devices: /device:TPU:66 before, /device:TPU:34 now
where the time goes in v1:
time: 140 us; the launch traced here: 139 us
  waiting for transfers between devices  63 us (45%)
  starting transfers between devices  40.3 us (29%)
  Pallas kernels  33.3 us (24%)
    ppermute x15, waiting for transfers between devices, send(): return lax.ppermute(value, 'dp', moves)  63 us
    pallas_call x5, Pallas kernels, stage(): pl.pallas_call(functools.partial(stage_kernel, plan), out_shape=shapes, i...  25.3 us
    ppermute x15, starting transfers between devices, send(): return lax.ppermute(value, 'dp', moves)  23 us
    all_to_all x1, starting transfers between devices, body(): lax.all_to_all(ring_part, 'dp', 0, 0, axis_index_groups=groups, tiled=True)  17.3 us
    pallas_call x1, Pallas kernels, normalize(): pl.pallas_call(unit_kernel, in_specs=[smem, smem, anywhere], out_specs=[a...  4.12 us
  transfers between devices with their start and end apart: 16, of which 8 were waited for; matrix products, arithmetic and copies ran while one was open for 0% of the time, Pallas kernels for 14%

profile of v1, /device:TPU:34, one launch (start us, length us, event | category | flops | bytes accessed | tf_op | source)
XLA Modules:
  0.0 138.6 jit_solution(12186312033319316568)
XLA Ops:
  0.7 4.1 %unit_rows.1 = (bf16[1040,1024]{1,0:T(8,128)(2,1)}, bf16[512,1024]{1,0:T(8,128)(2,1)}, bf16[512,1024]{1,0:T(8,128)(2,1)}) custom-call(s32[1,13]{1,0:T(1,128)} %list_ref.1, s32[1]{0:T(128)S(6)} %copy.4.count_ref, bf16[1024,1024]{1,0:T(8,128)(2,1)} %x_ref.1), custom_call_target="tpu_custom_call" | custom-call | tf_op jit(solution)/shard_map/unit_rows/pallas_call | solution.py:82
  4.8 3.0 %collective-permute-start.5 = (bf16[512,1024]{1,0:T(8,128)(2,1)}, bf16[512,1024]{1,0:T(8,128)(2,1)}, u32[]{:S(2)}, u32[]{:S(2)}) collective-permute-start(bf16[512,1024]{1,0:T(8,128)(2,1)} %get-tuple-element.48), channel_id=1, source_target_pairs={{16,24},{17,25},{18,26},{19,27},{20,28},{21,29},{22,30},{23,31},{2... | collective-permute-start | bytes 3145736 | tf_op jit(solution)/shard_map/ppermute | solution.py:45
  7.8 3.6 %collective-permute-start.4 = (bf16[1040,1024]{1,0:T(8,128)(2,1)}, bf16[1040,1024]{1,0:T(8,128)(2,1)}, u32[]{:S(2)}, u32[]{:S(2)}) collective-permute-start(bf16[1040,1024]{1,0:T(8,128)(2,1)} %get-tuple-element.51.refs_0_.refs_1_.refs_5_.refs_3_.refs_11_.refs_4_), channel_id=1, source_target_pairs={{8,0},{9,1},{10,2},{11,3},{12,4},{13,5},{14,6},{15,7},{16,8},{17,9... | collective-permute-start | bytes 6389768 | tf_op jit(solution)/shard_map/ppermute | solution.py:45
  11.4 0.5 collective-permute-start.1
  11.9 1.6 %collective-permute-start = (bf16[1040,1024]{1,0:T(8,128)(2,1)}, bf16[1040,1024]{1,0:T(8,128)(2,1)}, u32[]{:S(2)}, u32[]{:S(2)}) collective-permute-start(bf16[1040,1024]{1,0:T(8,128)(2,1)} %get-tuple-element.51.refs_0_.refs_1_.refs_5_.refs_3_.refs_11_.refs_4_), channel_id=1, source_target_pairs={{0,2},{1,3},{2,4},{3,5},{4,6},{5,7},{6,0},{7,1},{8,10},{9,11},{10,... | collective-permute-start | bytes 6389768 | tf_op jit(solution)/shard_map/ppermute | solution.py:45
  13.5 7.3 %own.1 = (f32[1,1024]{1,0:T(1,128)}, f32[1,1024]{1,0:T(1,128)}) custom-call(bf16[1040,1024]{1,0:T(8,128)(2,1)} %get-tuple-element.51.refs_0_.refs_1_.refs_5_.refs_3_.refs_11_.refs_4_, bf16[1040,1024]{1,0:T(8,128)(2,1)} %get-tuple-element.51.refs_0_.refs_1_.refs_5_.refs_3_.refs_11_.refs_4_), custom_call_target="tpu_custom_call" | custom-call | flops 8589934592 | bytes 1024 | tf_op jit(solution)/shard_map/own/pallas_call | solution.py:434
  20.8 12.3 %collective-permute-done.5 = bf16[512,1024]{1,0:T(8,128)(2,1)} collective-permute-done((bf16[512,1024]{1,0:T(8,128)(2,1)}, bf16[512,1024]{1,0:T(8,128)(2,1)}, u32[]{:S(2)}, u32[]{:S(2)}) %collective-permute-start.5) | collective-permute-done | bytes 1048608 | tf_op jit(solution)/shard_map/ppermute | solution.py:45
  33.2 0.0 collective-permute-start.7
  33.2 3.1 %collective-permute-start.6 = (bf16[512,1024]{1,0:T(8,128)(2,1)}, bf16[512,1024]{1,0:T(8,128)(2,1)}, u32[]{:S(2)}, u32[]{:S(2)}) collective-permute-start(bf16[512,1024]{1,0:T(8,128)(2,1)} %collective-permute-done.5), channel_id=1, source_target_pairs={{24,0},{25,1},{26,2},{27,3},{28,4},{29,5},{30,6},{31,7},{0,8},{1,9... | collective-permute-start | bytes 3145736 | tf_op jit(solution)/shard_map/ppermute | solution.py:45
  36.3 23.1 %collective-permute-done.1.b_ref.refs_4_.refs_6_ = bf16[1040,1024]{1,0:T(8,128)(2,1)} collective-permute-done((bf16[1040,1024]{1,0:T(8,128)(2,1)}, bf16[1040,1024]{1,0:T(8,128)(2,1)}, u32[]{:S(2)}, u32[]{:S(2)}) %collective-permute-start.1) | collective-permute-done | bytes 2129952 | tf_op jit(solution)/shard_map/ppermute | solution.py:45
  59.4 1.3 collective-permute-done.a_ref.refs_3_.refs_5_
  60.7 2.5 %halves.1 = (bf16[512,1024]{1,0:T(8,128)(2,1)}, bf16[528,1024]{1,0:T(8,128)(2,1)}) custom-call(bf16[1040,1024]{1,0:T(8,128)(2,1)} %collective-permute-done.a_ref.refs_3_.refs_5_, bf16[1040,1024]{1,0:T(8,128)(2,1)} %collective-permute-done.1.b_ref.refs_4_.refs_6_), custom_call_target="tpu_custom_call" | custom-call | tf_op jit(solution)/shard_map/halves/pallas_call | solution.py:122
  63.2 0.0 collective-permute-done.6.refs_7_.refs_5_.refs_13_.refs_6_
  63.2 0.0 collective-permute-done.4.refs_6_.refs_4_.refs_12_.refs_5_
  63.2 0.0 collective-permute-done.7.refs_2_.refs_4_
  63.2 0.1 collective-permute-start.9
  63.3 0.5 collective-permute-start.10
  63.8 2.9 %collective-permute-start.3 = (bf16[528,1024]{1,0:T(8,128)(2,1)}, bf16[528,1024]{1,0:T(8,128)(2,1)}, u32[]{:S(2)}, u32[]{:S(2)}) collective-permute-start(bf16[528,1024]{1,0:T(8,128)(2,1)} %get-tuple-element.46), channel_id=1, source_target_pairs={{0,6},{1,7},{2,0},{3,1},{4,2},{5,3},{6,4},{7,5},{8,14},{9,15},{10,... | collective-permute-start | bytes 3244040 | tf_op jit(solution)/shard_map/ppermute | solution.py:45
  66.7 0.0 collective-permute-start.2
  66.7 3.4 %collective-permute-start.8 = (bf16[512,1024]{1,0:T(8,128)(2,1)}, bf16[512,1024]{1,0:T(8,128)(2,1)}, u32[]{:S(2)}, u32[]{:S(2)}) collective-permute-start(bf16[512,1024]{1,0:T(8,128)(2,1)} %get-tuple-element.53), channel_id=1, source_target_pairs={{16,0},{17,1},{18,2},{19,3},{20,4},{21,5},{22,6},{23,7},{24,8},{25... | collective-permute-start | bytes 3145736 | tf_op jit(solution)/shard_map/ppermute | solution.py:45
  70.1 3.3 %near.1 = (f32[4,1024]{1,0:T(4,128)}, f32[3,1024]{1,0:T(4,128)}) custom-call(f32[1,1024]{1,0:T(1,128)} %get-tuple-element.54.refs_0_, bf16[1040,1024]{1,0:T(8,128)(2,1)} %get-tuple-element.51.refs_0_.refs_1_.refs_5_.refs_3_.refs_11_.refs_4_, bf16[1040,1024]{1,0:T(8,128)(2,1)} %collective-permute-done.7.refs_2_.refs_4_, ...), custom_call_target="tpu_custom_call" | custom-call | flops 1024 | bytes 1024 | tf_op jit(solution)/shard_map/near/pallas_call | solution.py:434
  73.4 0.0 collective-permute-done.9.refs_1_.refs_7_
  73.4 0.0 collective-permute-done.10.refs_2_.refs_8_
  73.4 2.9 %mid.1 = (f32[2,1024]{1,0:T(2,128)}, f32[3,1024]{1,0:T(4,128)}) custom-call(f32[3,1024]{1,0:T(4,128)} %get-tuple-element.60.refs_0_, bf16[1040,1024]{1,0:T(8,128)(2,1)} %collective-permute-done.9.refs_1_.refs_7_, bf16[1040,1024]{1,0:T(8,128)(2,1)} %collective-permute-done.10.refs_2_.refs_8_, ...), custom_call_target="tpu_custom_call" | custom-call | flops 1024 | bytes 1024 | tf_op jit(solution)/shard_map/mid/pallas_call | solution.py:434
  76.4 15.6 %collective-permute-done.2.refs_9_ = bf16[512,1024]{1,0:T(8,128)(2,1)} collective-permute-done((bf16[512,1024]{1,0:T(8,128)(2,1)}, bf16[512,1024]{1,0:T(8,128)(2,1)}, u32[]{:S(2)}, u32[]{:S(2)}) %collective-permute-start.2) | collective-permute-done | bytes 1048608 | tf_op jit(solution)/shard_map/ppermute | solution.py:45
  91.9 0.0 collective-permute-done.3.refs_10_
  91.9 3.4 %collective-permute-done.8.refs_14_.refs_7_ = bf16[512,1024]{1,0:T(8,128)(2,1)} collective-permute-done((bf16[512,1024]{1,0:T(8,128)(2,1)}, bf16[512,1024]{1,0:T(8,128)(2,1)}, u32[]{:S(2)}, u32[]{:S(2)}) %collective-permute-start.8) | collective-permute-done | bytes 1048608 | tf_op jit(solution)/shard_map/ppermute | solution.py:45
  95.3 0.0 collective-permute-start.11
  95.3 0.5 collective-permute-start.12
  95.8 3.7 %far.1 = (f32[7,1024]{1,0:T(8,128)}, f32[4,1024]{1,0:T(4,128)}) custom-call(f32[4,1024]{1,0:T(4,128)} %get-tuple-element.67.refs_0_, f32[2,1024]{1,0:T(2,128)} %get-tuple-element.68.refs_1_, f32[3,1024]{1,0:T(4,128)} %get-tuple-element.69.refs_2_, bf16[1040,1024]{1,0:T(8,128)(2,1)} %get-tuple-element.51.refs_0_.refs_1_.refs_5_.refs_3_.refs_11_.refs_4_, ...), custom_call_target="tpu_custom_call" | custom-call | flops 1024 | bytes 1024 | tf_op jit(solution)/shard_map/far/pallas_call | solution.py:434
  99.5 0.3 collective-permute-done.12.refs_2_
  99.9 0.0 collective-permute-done.11.refs_3_
  99.9 8.0 %last.1 = (f32[8,1,1024]{2,1,0:T(1,128)}, f32[1,1024]{1,0:T(1,128)}, f32[1,1024]{1,0:T(1,128)}) custom-call(f32[7,1024]{1,0:T(8,128)} %get-tuple-element.72.refs_0_, f32[4,1024]{1,0:T(4,128)} %get-tuple-element.73.refs_1_, bf16[512,1024]{1,0:T(8,128)(2,1)} %collective-permute-done.12.refs_2_, bf16[528,1024]{1,0:T(8,128)(2,1)} %collective-permute-done.11.refs_3_, ...), custom_call_target="tpu_custom_call" | custom-call | flops 1024 | bytes 1024 | tf_op jit(solution)/shard_map/last/pallas_call | solution.py:434
  107.9 17.3 %all-to-all-start = ((f32[8,1,1024]{2,1,0:T(1,128)}), f32[8,1,1024]{2,1,0:T(1,128)S(1)}, u32[]{:S(2)}, u32[]{:S(2)}) async-start(f32[8,1,1024]{2,1,0:T(1,128)} %get-tuple-element.76), calls=%async_computation | async-start | bytes 65536 | tf_op jit(solution)/shard_map/all_to_all | solution.py:538
  125.2 1.9 %collective-permute-start.13 = (f32[1,1024]{1,0:T(1,128)}, f32[1,1024]{1,0:T(1,128)S(1)}, u32[]{:S(2)}, u32[]{:S(2)}) collective-permute-start(f32[1,1024]{1,0:T(1,128)} %get-tuple-element.77), channel_id=1, source_target_pairs={{0,8},{1,9},{2,10},{3,11},{4,12},{5,13},{6,14},{7,15},{8,16},{9,17... | collective-permute-start | bytes 12296 | tf_op jit(solution)/shard_map/ppermute | solution.py:45
  127.1 1.9 %collective-permute-start.14 = (f32[1,1024]{1,0:T(1,128)}, f32[1,1024]{1,0:T(1,128)S(1)}, u32[]{:S(2)}, u32[]{:S(2)}) collective-permute-start(f32[1,1024]{1,0:T(1,128)} %get-tuple-element.78), channel_id=1, source_target_pairs={{0,16},{1,17},{2,18},{3,19},{4,20},{5,21},{6,22},{7,23},{8,24},{9,... | collective-permute-start | bytes 12296 | tf_op jit(solution)/shard_map/ppermute | solution.py:45
  129.0 4.0 %collective-permute-done.13.refs_0_ = f32[1,1024]{1,0:T(1,128)S(1)} collective-permute-done((f32[1,1024]{1,0:T(1,128)}, f32[1,1024]{1,0:T(1,128)S(1)}, u32[]{:S(2)}, u32[]{:S(2)}) %collective-permute-start.13) | collective-permute-done | bytes 4128 | tf_op jit(solution)/shard_map/ppermute | solution.py:45
  133.0 0.0 copy-start.1
  133.0 3.0 %collective-permute-done.14.refs_1_ = f32[1,1024]{1,0:T(1,128)S(1)} collective-permute-done((f32[1,1024]{1,0:T(1,128)}, f32[1,1024]{1,0:T(1,128)S(1)}, u32[]{:S(2)}, u32[]{:S(2)}) %collective-permute-start.14) | collective-permute-done | bytes 4128 | tf_op jit(solution)/shard_map/ppermute | solution.py:45
  136.0 0.0 copy-start.2
  136.0 0.0 all-to-all-done.ring_ref
  136.0 0.0 copy-done.1
  136.0 0.6 copy-done.2
  136.6 0.0 copy-start
  136.6 0.6 copy-done
  137.2 1.4 %last_sum.1 = f32[1,1024]{1,0:T(1,128)} custom-call(f32[8,1,1024]{2,1,0:T(1,128)} %copy-done, f32[1,1024]{1,0:T(1,128)} %copy-done.1, f32[1,1024]{1,0:T(1,128)} %copy-done.2), custom_call_target="tpu_custom_call" | custom-call | tf_op jit(solution)/shard_map/last_sum/pallas_call | solution.py:539
Async XLA Ops:
  4.8 28.4 %collective-permute-start.5 = (bf16[512,1024]{1,0:T(8,128)(2,1)}, bf16[512,1024]{1,0:T(8,128)(2,1)}, u32[]{:S(2)}, u32[]{:S(2)}) collective-permute-start(bf16[512,1024]{1,0:T(8,128)(2,1)} %get-tuple-element.48), channel_id=1, source_target_pairs={{16,24},{17,25},{18,26},{19,27},{20,28},{21,29},{22,30},{23,31},{2... | collective-permute-start | bytes 3145736 | tf_op jit(solution)/shard_map/ppermute | solution.py:45
  7.8 55.4 %collective-permute-start.4 = (bf16[1040,1024]{1,0:T(8,128)(2,1)}, bf16[1040,1024]{1,0:T(8,128)(2,1)}, u32[]{:S(2)}, u32[]{:S(2)}) collective-permute-start(bf16[1040,1024]{1,0:T(8,128)(2,1)} %get-tuple-element.51.refs_0_.refs_1_.refs_5_.refs_3_.refs_11_.refs_4_), channel_id=1, source_target_pairs={{8,0},{9,1},{10,2},{11,3},{12,4},{13,5},{14,6},{15,7},{16,8},{17,9... | collective-permute-start | bytes 6389768 | tf_op jit(solution)/shard_map/ppermute | solution.py:45
  11.4 48.0 %collective-permute-start.1 = (bf16[1040,1024]{1,0:T(8,128)(2,1)}, bf16[1040,1024]{1,0:T(8,128)(2,1)}, u32[]{:S(2)}, u32[]{:S(2)}) collective-permute-start(bf16[1040,1024]{1,0:T(8,128)(2,1)} %get-tuple-element.51.refs_0_.refs_1_.refs_5_.refs_3_.refs_11_.refs_4_), channel_id=1, source_target_pairs={{0,6},{1,7},{2,0},{3,1},{4,2},{5,3},{6,4},{7,5},{8,14},{9,15},{10,... | collective-permute-start | bytes 6389768 | tf_op jit(solution)/shard_map/ppermute | solution.py:45
  11.9 48.7 %collective-permute-start = (bf16[1040,1024]{1,0:T(8,128)(2,1)}, bf16[1040,1024]{1,0:T(8,128)(2,1)}, u32[]{:S(2)}, u32[]{:S(2)}) collective-permute-start(bf16[1040,1024]{1,0:T(8,128)(2,1)} %get-tuple-element.51.refs_0_.refs_1_.refs_5_.refs_3_.refs_11_.refs_4_), channel_id=1, source_target_pairs={{0,2},{1,3},{2,4},{3,5},{4,6},{5,7},{6,0},{7,1},{8,10},{9,11},{10,... | collective-permute-start | bytes 6389768 | tf_op jit(solution)/shard_map/ppermute | solution.py:45
  33.2 30.0 %collective-permute-start.7 = (bf16[1040,1024]{1,0:T(8,128)(2,1)}, bf16[1040,1024]{1,0:T(8,128)(2,1)}, u32[]{:S(2)}, u32[]{:S(2)}) collective-permute-start(bf16[1040,1024]{1,0:T(8,128)(2,1)} %get-tuple-element.51.refs_0_.refs_1_.refs_5_.refs_3_.refs_11_.refs_4_), channel_id=1, source_target_pairs={{0,1},{1,0},{2,3},{3,2},{4,5},{5,4},{6,7},{7,6},{8,9},{9,8},{10,11... | collective-permute-start | bytes 6389768 | tf_op jit(solution)/shard_map/ppermute | solution.py:45
  33.2 30.0 %collective-permute-start.6 = (bf16[512,1024]{1,0:T(8,128)(2,1)}, bf16[512,1024]{1,0:T(8,128)(2,1)}, u32[]{:S(2)}, u32[]{:S(2)}) collective-permute-start(bf16[512,1024]{1,0:T(8,128)(2,1)} %collective-permute-done.5), channel_id=1, source_target_pairs={{24,0},{25,1},{26,2},{27,3},{28,4},{29,5},{30,6},{31,7},{0,8},{1,9... | collective-permute-start | bytes 3145736 | tf_op jit(solution)/shard_map/ppermute | solution.py:45
  63.2 10.2 %collective-permute-start.9 = (bf16[1040,1024]{1,0:T(8,128)(2,1)}, bf16[1040,1024]{1,0:T(8,128)(2,1)}, u32[]{:S(2)}, u32[]{:S(2)}) collective-permute-start(bf16[1040,1024]{1,0:T(8,128)(2,1)} %collective-permute-done.a_ref.refs_3_.refs_5_), channel_id=1, source_target_pairs={{0,1},{1,0},{2,3},{3,2},{4,5},{5,4},{6,7},{7,6},{8,9},{9,8},{10,11... | collective-permute-start | bytes 6389768 | tf_op jit(solution)/shard_map/ppermute | solution.py:45
  63.3 10.1 %collective-permute-start.10 = (bf16[1040,1024]{1,0:T(8,128)(2,1)}, bf16[1040,1024]{1,0:T(8,128)(2,1)}, u32[]{:S(2)}, u32[]{:S(2)}) collective-permute-start(bf16[1040,1024]{1,0:T(8,128)(2,1)} %collective-permute-done.1.b_ref.refs_4_.refs_6_), channel_id=1, source_target_pairs={{0,1},{1,0},{2,3},{3,2},{4,5},{5,4},{6,7},{7,6},{8,9},{9,8},{10,11... | collective-permute-start | bytes 6389768 | tf_op jit(solution)/shard_map/ppermute | solution.py:45
  63.8 28.1 %collective-permute-start.3 = (bf16[528,1024]{1,0:T(8,128)(2,1)}, bf16[528,1024]{1,0:T(8,128)(2,1)}, u32[]{:S(2)}, u32[]{:S(2)}) collective-permute-start(bf16[528,1024]{1,0:T(8,128)(2,1)} %get-tuple-element.46), channel_id=1, source_target_pairs={{0,6},{1,7},{2,0},{3,1},{4,2},{5,3},{6,4},{7,5},{8,14},{9,15},{10,... | collective-permute-start | bytes 3244040 | tf_op jit(solution)/shard_map/ppermute | solution.py:45
  66.7 25.2 %collective-permute-start.2 = (bf16[512,1024]{1,0:T(8,128)(2,1)}, bf16[512,1024]{1,0:T(8,128)(2,1)}, u32[]{:S(2)}, u32[]{:S(2)}) collective-permute-start(bf16[512,1024]{1,0:T(8,128)(2,1)} %get-tuple-element.45), channel_id=1, source_target_pairs={{0,2},{1,3},{2,4},{3,5},{4,6},{5,7},{6,0},{7,1},{8,10},{9,11},{10,... | collective-permute-start | bytes 3145736 | tf_op jit(solution)/shard_map/ppermute | solution.py:45
  66.7 28.6 %collective-permute-start.8 = (bf16[512,1024]{1,0:T(8,128)(2,1)}, bf16[512,1024]{1,0:T(8,128)(2,1)}, u32[]{:S(2)}, u32[]{:S(2)}) collective-permute-start(bf16[512,1024]{1,0:T(8,128)(2,1)} %get-tuple-element.53), channel_id=1, source_target_pairs={{16,0},{17,1},{18,2},{19,3},{20,4},{21,5},{22,6},{23,7},{24,8},{25... | collective-permute-start | bytes 3145736 | tf_op jit(solution)/shard_map/ppermute | solution.py:45
  95.3 4.6 %collective-permute-start.11 = (bf16[528,1024]{1,0:T(8,128)(2,1)}, bf16[528,1024]{1,0:T(8,128)(2,1)}, u32[]{:S(2)}, u32[]{:S(2)}) collective-permute-start(bf16[528,1024]{1,0:T(8,128)(2,1)} %collective-permute-done.3.refs_10_), channel_id=1, source_target_pairs={{0,1},{1,0},{2,3},{3,2},{4,5},{5,4},{6,7},{7,6},{8,9},{9,8},{10,11... | collective-permute-start | bytes 3244040 | tf_op jit(solution)/shard_map/ppermute | solution.py:45
  95.3 4.5 %collective-permute-start.12 = (bf16[512,1024]{1,0:T(8,128)(2,1)}, bf16[512,1024]{1,0:T(8,128)(2,1)}, u32[]{:S(2)}, u32[]{:S(2)}) collective-permute-start(bf16[512,1024]{1,0:T(8,128)(2,1)} %collective-permute-done.2.refs_9_), channel_id=1, source_target_pairs={{0,1},{1,0},{2,3},{3,2},{4,5},{5,4},{6,7},{7,6},{8,9},{9,8},{10,11... | collective-permute-start | bytes 3145736 | tf_op jit(solution)/shard_map/ppermute | solution.py:45
  107.9 28.1 %all-to-all-start = ((f32[8,1,1024]{2,1,0:T(1,128)}), f32[8,1,1024]{2,1,0:T(1,128)S(1)}, u32[]{:S(2)}, u32[]{:S(2)}) async-start(f32[8,1,1024]{2,1,0:T(1,128)} %get-tuple-element.76), calls=%async_computation | async-start | bytes 65536 | tf_op jit(solution)/shard_map/all_to_all | solution.py:538
  125.2 7.8 %collective-permute-start.13 = (f32[1,1024]{1,0:T(1,128)}, f32[1,1024]{1,0:T(1,128)S(1)}, u32[]{:S(2)}, u32[]{:S(2)}) collective-permute-start(f32[1,1024]{1,0:T(1,128)} %get-tuple-element.77), channel_id=1, source_target_pairs={{0,8},{1,9},{2,10},{3,11},{4,12},{5,13},{6,14},{7,15},{8,16},{9,17... | collective-permute-start | bytes 12296 | tf_op jit(solution)/shard_map/ppermute | solution.py:45
  127.1 8.9 %collective-permute-start.14 = (f32[1,1024]{1,0:T(1,128)}, f32[1,1024]{1,0:T(1,128)S(1)}, u32[]{:S(2)}, u32[]{:S(2)}) collective-permute-start(f32[1,1024]{1,0:T(1,128)} %get-tuple-element.78), channel_id=1, source_target_pairs={{0,16},{1,17},{2,18},{3,19},{4,20},{5,21},{6,22},{7,23},{8,24},{9,... | collective-permute-start | bytes 12296 | tf_op jit(solution)/shard_map/ppermute | solution.py:45
  133.0 3.0 %copy-start.1 = (f32[1,1024]{1,0:T(1,128)}, f32[1,1024]{1,0:T(1,128)S(1)}, u32[]{:S(2)}) copy-start(f32[1,1024]{1,0:T(1,128)S(1)} %collective-permute-done.13.refs_0_) | copy-start | bytes 12292
  136.0 0.6 copy-start.2
  136.6 0.6 copy-start

commit v2 on v1

--- a/solution.py
+++ b/solution.py
@@ -308,7 +308,7 @@
                     col_s[r, :, :width] = total
                 return 0
 
-            lax.fori_loop(0, B // G, group, 0)
+            lax.fori_loop(0, B // G, group, 0, unroll=4)
 
     def arrive(r):
         @pl.when(waited[r] == 0)

time: 140 us -> 143 us (1.021); the launches traced: 139 us -> 143 us
  starting transfers between devices: 40.3 us -> 44.4 us
    ppermute x15, starting transfers between devices: 23 us -> 30.3 us  [send(): return lax.ppermute(value, 'dp', moves)]
    all_to_all x1, starting transfers between devices: 17.3 us -> 14.1 us  [body(): lax.all_to_all(ring_part, 'dp', 0, 0, axis_index_groups=groups, tiled=True)]
  transfers between devices with their start and end apart: 16 -> 16, of which waited for: 8 -> 6; matrix products, arithmetic and copies ran while one was open for 0% -> 0% of each run, Pallas kernels for 14% -> 18%
where the time goes in v2:
time: 143 us
  waiting for transfers between devices  62.3 us (44%)
  starting transfers between devices  44.4 us (31%)
  Pallas kernels  34.7 us (24%)
    ppermute x15, waiting for transfers between devices, send(): return lax.ppermute(value, 'dp', moves)  62.3 us
    ppermute x15, starting transfers between devices, send(): return lax.ppermute(value, 'dp', moves)  30.3 us
    pallas_call x5, Pallas kernels, stage(): pl.pallas_call(functools.partial(stage_kernel, plan), out_shape=shapes, i...  26.6 us
    all_to_all x1, starting transfers between devices, body(): lax.all_to_all(ring_part, 'dp', 0, 0, axis_index_groups=groups, tiled=True)  14.1 us
    pallas_call x1, Pallas kernels, normalize(): pl.pallas_call(unit_kernel, in_specs=[smem, smem, anywhere], out_specs=[a...  4.12 us
  transfers between devices with their start and end apart: 16, of which 6 were waited for; matrix products, arithmetic and copies ran while one was open for 0% of the time, Pallas kernels for 18%

profile of v2, /device:TPU:34, one launch (start us, length us, event | category | flops | bytes accessed | tf_op | source)
XLA Modules:
  0.0 143.4 jit_solution(771300731898402008)
XLA Ops:
  0.7 4.1 %unit_rows.1 = (bf16[1040,1024]{1,0:T(8,128)(2,1)}, bf16[512,1024]{1,0:T(8,128)(2,1)}, bf16[512,1024]{1,0:T(8,128)(2,1)}) custom-call(s32[1,13]{1,0:T(1,128)} %list_ref.1, s32[1]{0:T(128)S(6)} %copy.4.count_ref, bf16[1024,1024]{1,0:T(8,128)(2,1)} %x_ref.1), custom_call_target="tpu_custom_call" | custom-call | tf_op jit(solution)/shard_map/unit_rows/pallas_call | solution.py:82
  4.8 3.0 %collective-permute-start.5 = (bf16[512,1024]{1,0:T(8,128)(2,1)}, bf16[512,1024]{1,0:T(8,128)(2,1)}, u32[]{:S(2)}, u32[]{:S(2)}) collective-permute-start(bf16[512,1024]{1,0:T(8,128)(2,1)} %get-tuple-element.48), channel_id=1, source_target_pairs={{16,24},{17,25},{18,26},{19,27},{20,28},{21,29},{22,30},{23,31},{2... | collective-permute-start | bytes 3145736 | tf_op jit(solution)/shard_map/ppermute | solution.py:45
  7.8 3.6 %collective-permute-start.4 = (bf16[1040,1024]{1,0:T(8,128)(2,1)}, bf16[1040,1024]{1,0:T(8,128)(2,1)}, u32[]{:S(2)}, u32[]{:S(2)}) collective-permute-start(bf16[1040,1024]{1,0:T(8,128)(2,1)} %get-tuple-element.51.refs_0_.refs_1_.refs_5_.refs_3_.refs_11_.refs_4_), channel_id=1, source_target_pairs={{8,0},{9,1},{10,2},{11,3},{12,4},{13,5},{14,6},{15,7},{16,8},{17,9... | collective-permute-start | bytes 6389768 | tf_op jit(solution)/shard_map/ppermute | solution.py:45
  11.4 0.5 collective-permute-start.1
  11.9 1.6 %collective-permute-start = (bf16[1040,1024]{1,0:T(8,128)(2,1)}, bf16[1040,1024]{1,0:T(8,128)(2,1)}, u32[]{:S(2)}, u32[]{:S(2)}) collective-permute-start(bf16[1040,1024]{1,0:T(8,128)(2,1)} %get-tuple-element.51.refs_0_.refs_1_.refs_5_.refs_3_.refs_11_.refs_4_), channel_id=1, source_target_pairs={{0,2},{1,3},{2,4},{3,5},{4,6},{5,7},{6,0},{7,1},{8,10},{9,11},{10,... | collective-permute-start | bytes 6389768 | tf_op jit(solution)/shard_map/ppermute | solution.py:45
  13.5 6.9 %own.1 = (f32[1,1024]{1,0:T(1,128)}, f32[1,1024]{1,0:T(1,128)}) custom-call(bf16[1040,1024]{1,0:T(8,128)(2,1)} %get-tuple-element.51.refs_0_.refs_1_.refs_5_.refs_3_.refs_11_.refs_4_, bf16[1040,1024]{1,0:T(8,128)(2,1)} %get-tuple-element.51.refs_0_.refs_1_.refs_5_.refs_3_.refs_11_.refs_4_), custom_call_target="tpu_custom_call" | custom-call | flops 8589934592 | bytes 1024 | tf_op jit(solution)/shard_map/own/pallas_call | solution.py:434
  20.4 12.8 %collective-permute-done.5 = bf16[512,1024]{1,0:T(8,128)(2,1)} collective-permute-done((bf16[512,1024]{1,0:T(8,128)(2,1)}, bf16[512,1024]{1,0:T(8,128)(2,1)}, u32[]{:S(2)}, u32[]{:S(2)}) %collective-permute-start.5) | collective-permute-done | bytes 1048608 | tf_op jit(solution)/shard_map/ppermute | solution.py:45
  33.2 0.0 collective-permute-start.7
  33.2 3.1 %collective-permute-start.6 = (bf16[512,1024]{1,0:T(8,128)(2,1)}, bf16[512,1024]{1,0:T(8,128)(2,1)}, u32[]{:S(2)}, u32[]{:S(2)}) collective-permute-start(bf16[512,1024]{1,0:T(8,128)(2,1)} %collective-permute-done.5), channel_id=1, source_target_pairs={{24,0},{25,1},{26,2},{27,3},{28,4},{29,5},{30,6},{31,7},{0,8},{1,9... | collective-permute-start | bytes 3145736 | tf_op jit(solution)/shard_map/ppermute | solution.py:45
  36.3 23.1 %collective-permute-done.1.b_ref.refs_4_.refs_6_ = bf16[1040,1024]{1,0:T(8,128)(2,1)} collective-permute-done((bf16[1040,1024]{1,0:T(8,128)(2,1)}, bf16[1040,1024]{1,0:T(8,128)(2,1)}, u32[]{:S(2)}, u32[]{:S(2)}) %collective-permute-start.1) | collective-permute-done | bytes 2129952 | tf_op jit(solution)/shard_map/ppermute | solution.py:45
  59.4 1.3 collective-permute-done.a_ref.refs_3_.refs_5_
  60.7 2.5 %halves.1 = (bf16[512,1024]{1,0:T(8,128)(2,1)}, bf16[528,1024]{1,0:T(8,128)(2,1)}) custom-call(bf16[1040,1024]{1,0:T(8,128)(2,1)} %collective-permute-done.a_ref.refs_3_.refs_5_, bf16[1040,1024]{1,0:T(8,128)(2,1)} %collective-permute-done.1.b_ref.refs_4_.refs_6_), custom_call_target="tpu_custom_call" | custom-call | tf_op jit(solution)/shard_map/halves/pallas_call | solution.py:122
  63.2 0.0 collective-permute-done.6.refs_7_.refs_5_.refs_13_.refs_6_
  63.2 0.0 collective-permute-done.4.refs_6_.refs_4_.refs_12_.refs_5_
  63.2 0.0 collective-permute-done.7.refs_2_.refs_4_
  63.2 0.1 collective-permute-start.9
  63.3 0.5 collective-permute-start.10
  63.8 2.9 %collective-permute-start.3 = (bf16[528,1024]{1,0:T(8,128)(2,1)}, bf16[528,1024]{1,0:T(8,128)(2,1)}, u32[]{:S(2)}, u32[]{:S(2)}) collective-permute-start(bf16[528,1024]{1,0:T(8,128)(2,1)} %get-tuple-element.46), channel_id=1, source_target_pairs={{0,6},{1,7},{2,0},{3,1},{4,2},{5,3},{6,4},{7,5},{8,14},{9,15},{10,... | collective-permute-start | bytes 3244040 | tf_op jit(solution)/shard_map/ppermute | solution.py:45
  66.7 0.0 collective-permute-start.2
  66.7 3.4 %collective-permute-start.8 = (bf16[512,1024]{1,0:T(8,128)(2,1)}, bf16[512,1024]{1,0:T(8,128)(2,1)}, u32[]{:S(2)}, u32[]{:S(2)}) collective-permute-start(bf16[512,1024]{1,0:T(8,128)(2,1)} %get-tuple-element.53), channel_id=1, source_target_pairs={{16,0},{17,1},{18,2},{19,3},{20,4},{21,5},{22,6},{23,7},{24,8},{25... | collective-permute-start | bytes 3145736 | tf_op jit(solution)/shard_map/ppermute | solution.py:45
  70.1 3.3 %near.1 = (f32[4,1024]{1,0:T(4,128)}, f32[3,1024]{1,0:T(4,128)}) custom-call(f32[1,1024]{1,0:T(1,128)} %get-tuple-element.54.refs_0_, bf16[1040,1024]{1,0:T(8,128)(2,1)} %get-tuple-element.51.refs_0_.refs_1_.refs_5_.refs_3_.refs_11_.refs_4_, bf16[1040,1024]{1,0:T(8,128)(2,1)} %collective-permute-done.7.refs_2_.refs_4_, ...), custom_call_target="tpu_custom_call" | custom-call | flops 1024 | bytes 1024 | tf_op jit(solution)/shard_map/near/pallas_call | solution.py:434
  73.4 0.0 collective-permute-done.9.refs_1_.refs_7_
  73.4 0.0 collective-permute-done.10.refs_2_.refs_8_
  73.4 2.9 %mid.1 = (f32[2,1024]{1,0:T(2,128)}, f32[3,1024]{1,0:T(4,128)}) custom-call(f32[3,1024]{1,0:T(4,128)} %get-tuple-element.60.refs_0_, bf16[1040,1024]{1,0:T(8,128)(2,1)} %collective-permute-done.9.refs_1_.refs_7_, bf16[1040,1024]{1,0:T(8,128)(2,1)} %collective-permute-done.10.refs_2_.refs_8_, ...), custom_call_target="tpu_custom_call" | custom-call | flops 1024 | bytes 1024 | tf_op jit(solution)/shard_map/mid/pallas_call | solution.py:434
  76.4 15.6 %collective-permute-done.2.refs_9_ = bf16[512,1024]{1,0:T(8,128)(2,1)} collective-permute-done((bf16[512,1024]{1,0:T(8,128)(2,1)}, bf16[512,1024]{1,0:T(8,128)(2,1)}, u32[]{:S(2)}, u32[]{:S(2)}) %collective-permute-start.2) | collective-permute-done | bytes 1048608 | tf_op jit(solution)/shard_map/ppermute | solution.py:45
  91.9 0.0 collective-permute-done.3.refs_10_
  91.9 3.4 %collective-permute-done.8.refs_14_.refs_7_ = bf16[512,1024]{1,0:T(8,128)(2,1)} collective-permute-done((bf16[512,1024]{1,0:T(8,128)(2,1)}, bf16[512,1024]{1,0:T(8,128)(2,1)}, u32[]{:S(2)}, u32[]{:S(2)}) %collective-permute-start.8) | collective-permute-done | bytes 1048608 | tf_op jit(solution)/shard_map/ppermute | solution.py:45
  95.3 0.0 collective-permute-start.11
  95.3 0.5 collective-permute-start.12
  95.8 10.6 %far.1 = (f32[7,1024]{1,0:T(8,128)}, f32[4,1024]{1,0:T(4,128)}) custom-call(f32[4,1024]{1,0:T(4,128)} %get-tuple-element.67.refs_0_, f32[2,1024]{1,0:T(2,128)} %get-tuple-element.68.refs_1_, f32[3,1024]{1,0:T(4,128)} %get-tuple-element.69.refs_2_, bf16[1040,1024]{1,0:T(8,128)(2,1)} %get-tuple-element.51.refs_0_.refs_1_.refs_5_.refs_3_.refs_11_.refs_4_, ...), custom_call_target="tpu_custom_call" | custom-call | flops 1024 | bytes 1024 | tf_op jit(solution)/shard_map/far/pallas_call | solution.py:434
  106.4 0.0 collective-permute-done.12.refs_2_
  106.4 0.0 collective-permute-done.11.refs_3_
  106.4 2.9 %last.1 = (f32[8,1,1024]{2,1,0:T(1,128)}, f32[1,1024]{1,0:T(1,128)}, f32[1,1024]{1,0:T(1,128)}) custom-call(f32[7,1024]{1,0:T(8,128)} %get-tuple-element.72.refs_0_, f32[4,1024]{1,0:T(4,128)} %get-tuple-element.73.refs_1_, bf16[512,1024]{1,0:T(8,128)(2,1)} %collective-permute-done.12.refs_2_, bf16[528,1024]{1,0:T(8,128)(2,1)} %collective-permute-done.11.refs_3_, ...), custom_call_target="tpu_custom_call" | custom-call | flops 1024 | bytes 1024 | tf_op jit(solution)/shard_map/last/pallas_call | solution.py:434
  109.3 14.1 %all-to-all-start = ((f32[8,1,1024]{2,1,0:T(1,128)}), f32[8,1,1024]{2,1,0:T(1,128)S(1)}, u32[]{:S(2)}, u32[]{:S(2)}) async-start(f32[8,1,1024]{2,1,0:T(1,128)} %get-tuple-element.76), calls=%async_computation | async-start | bytes 65536 | tf_op jit(solution)/shard_map/all_to_all | solution.py:538
  123.4 9.3 %collective-permute-start.13 = (f32[1,1024]{1,0:T(1,128)}, f32[1,1024]{1,0:T(1,128)S(1)}, u32[]{:S(2)}, u32[]{:S(2)}) collective-permute-start(f32[1,1024]{1,0:T(1,128)} %get-tuple-element.77), channel_id=1, source_target_pairs={{0,8},{1,9},{2,10},{3,11},{4,12},{5,13},{6,14},{7,15},{8,16},{9,17... | collective-permute-start | bytes 12296 | tf_op jit(solution)/shard_map/ppermute | solution.py:45
  132.7 1.9 %collective-permute-start.14 = (f32[1,1024]{1,0:T(1,128)}, f32[1,1024]{1,0:T(1,128)S(1)}, u32[]{:S(2)}, u32[]{:S(2)}) collective-permute-start(f32[1,1024]{1,0:T(1,128)} %get-tuple-element.78), channel_id=1, source_target_pairs={{0,16},{1,17},{2,18},{3,19},{4,20},{5,21},{6,22},{7,23},{8,24},{9,... | collective-permute-start | bytes 12296 | tf_op jit(solution)/shard_map/ppermute | solution.py:45
  134.6 0.0 collective-permute-done.13.refs_0_
  134.6 0.0 copy-start.1
  134.6 6.2 %collective-permute-done.14.refs_1_ = f32[1,1024]{1,0:T(1,128)S(1)} collective-permute-done((f32[1,1024]{1,0:T(1,128)}, f32[1,1024]{1,0:T(1,128)S(1)}, u32[]{:S(2)}, u32[]{:S(2)}) %collective-permute-start.14) | collective-permute-done | bytes 4128 | tf_op jit(solution)/shard_map/ppermute | solution.py:45
  140.8 0.0 copy-start.2
  140.8 0.0 all-to-all-done.ring_ref
  140.8 0.0 copy-done.1
  140.8 0.6 copy-done.2
  141.4 0.0 copy-start
  141.4 0.6 copy-done
  142.0 1.4 last_sum.1
Async XLA Ops:
  4.8 28.4 %collective-permute-start.5 = (bf16[512,1024]{1,0:T(8,128)(2,1)}, bf16[512,1024]{1,0:T(8,128)(2,1)}, u32[]{:S(2)}, u32[]{:S(2)}) collective-permute-start(bf16[512,1024]{1,0:T(8,128)(2,1)} %get-tuple-element.48), channel_id=1, source_target_pairs={{16,24},{17,25},{18,26},{19,27},{20,28},{21,29},{22,30},{23,31},{2... | collective-permute-start | bytes 3145736 | tf_op jit(solution)/shard_map/ppermute | solution.py:45
  7.8 55.4 %collective-permute-start.4 = (bf16[1040,1024]{1,0:T(8,128)(2,1)}, bf16[1040,1024]{1,0:T(8,128)(2,1)}, u32[]{:S(2)}, u32[]{:S(2)}) collective-permute-start(bf16[1040,1024]{1,0:T(8,128)(2,1)} %get-tuple-element.51.refs_0_.refs_1_.refs_5_.refs_3_.refs_11_.refs_4_), channel_id=1, source_target_pairs={{8,0},{9,1},{10,2},{11,3},{12,4},{13,5},{14,6},{15,7},{16,8},{17,9... | collective-permute-start | bytes 6389768 | tf_op jit(solution)/shard_map/ppermute | solution.py:45
  11.4 48.0 %collective-permute-start.1 = (bf16[1040,1024]{1,0:T(8,128)(2,1)}, bf16[1040,1024]{1,0:T(8,128)(2,1)}, u32[]{:S(2)}, u32[]{:S(2)}) collective-permute-start(bf16[1040,1024]{1,0:T(8,128)(2,1)} %get-tuple-element.51.refs_0_.refs_1_.refs_5_.refs_3_.refs_11_.refs_4_), channel_id=1, source_target_pairs={{0,6},{1,7},{2,0},{3,1},{4,2},{5,3},{6,4},{7,5},{8,14},{9,15},{10,... | collective-permute-start | bytes 6389768 | tf_op jit(solution)/shard_map/ppermute | solution.py:45
  11.9 48.7 %collective-permute-start = (bf16[1040,1024]{1,0:T(8,128)(2,1)}, bf16[1040,1024]{1,0:T(8,128)(2,1)}, u32[]{:S(2)}, u32[]{:S(2)}) collective-permute-start(bf16[1040,1024]{1,0:T(8,128)(2,1)} %get-tuple-element.51.refs_0_.refs_1_.refs_5_.refs_3_.refs_11_.refs_4_), channel_id=1, source_target_pairs={{0,2},{1,3},{2,4},{3,5},{4,6},{5,7},{6,0},{7,1},{8,10},{9,11},{10,... | collective-permute-start | bytes 6389768 | tf_op jit(solution)/shard_map/ppermute | solution.py:45
  33.2 30.0 %collective-permute-start.7 = (bf16[1040,1024]{1,0:T(8,128)(2,1)}, bf16[1040,1024]{1,0:T(8,128)(2,1)}, u32[]{:S(2)}, u32[]{:S(2)}) collective-permute-start(bf16[1040,1024]{1,0:T(8,128)(2,1)} %get-tuple-element.51.refs_0_.refs_1_.refs_5_.refs_3_.refs_11_.refs_4_), channel_id=1, source_target_pairs={{0,1},{1,0},{2,3},{3,2},{4,5},{5,4},{6,7},{7,6},{8,9},{9,8},{10,11... | collective-permute-start | bytes 6389768 | tf_op jit(solution)/shard_map/ppermute | solution.py:45
  33.2 30.0 %collective-permute-start.6 = (bf16[512,1024]{1,0:T(8,128)(2,1)}, bf16[512,1024]{1,0:T(8,128)(2,1)}, u32[]{:S(2)}, u32[]{:S(2)}) collective-permute-start(bf16[512,1024]{1,0:T(8,128)(2,1)} %collective-permute-done.5), channel_id=1, source_target_pairs={{24,0},{25,1},{26,2},{27,3},{28,4},{29,5},{30,6},{31,7},{0,8},{1,9... | collective-permute-start | bytes 3145736 | tf_op jit(solution)/shard_map/ppermute | solution.py:45
  63.2 10.2 %collective-permute-start.9 = (bf16[1040,1024]{1,0:T(8,128)(2,1)}, bf16[1040,1024]{1,0:T(8,128)(2,1)}, u32[]{:S(2)}, u32[]{:S(2)}) collective-permute-start(bf16[1040,1024]{1,0:T(8,128)(2,1)} %collective-permute-done.a_ref.refs_3_.refs_5_), channel_id=1, source_target_pairs={{0,1},{1,0},{2,3},{3,2},{4,5},{5,4},{6,7},{7,6},{8,9},{9,8},{10,11... | collective-permute-start | bytes 6389768 | tf_op jit(solution)/shard_map/ppermute | solution.py:45
  63.3 10.1 %collective-permute-start.10 = (bf16[1040,1024]{1,0:T(8,128)(2,1)}, bf16[1040,1024]{1,0:T(8,128)(2,1)}, u32[]{:S(2)}, u32[]{:S(2)}) collective-permute-start(bf16[1040,1024]{1,0:T(8,128)(2,1)} %collective-permute-done.1.b_ref.refs_4_.refs_6_), channel_id=1, source_target_pairs={{0,1},{1,0},{2,3},{3,2},{4,5},{5,4},{6,7},{7,6},{8,9},{9,8},{10,11... | collective-permute-start | bytes 6389768 | tf_op jit(solution)/shard_map/ppermute | solution.py:45
  63.8 28.1 %collective-permute-start.3 = (bf16[528,1024]{1,0:T(8,128)(2,1)}, bf16[528,1024]{1,0:T(8,128)(2,1)}, u32[]{:S(2)}, u32[]{:S(2)}) collective-permute-start(bf16[528,1024]{1,0:T(8,128)(2,1)} %get-tuple-element.46), channel_id=1, source_target_pairs={{0,6},{1,7},{2,0},{3,1},{4,2},{5,3},{6,4},{7,5},{8,14},{9,15},{10,... | collective-permute-start | bytes 3244040 | tf_op jit(solution)/shard_map/ppermute | solution.py:45
  66.7 25.2 %collective-permute-start.2 = (bf16[512,1024]{1,0:T(8,128)(2,1)}, bf16[512,1024]{1,0:T(8,128)(2,1)}, u32[]{:S(2)}, u32[]{:S(2)}) collective-permute-start(bf16[512,1024]{1,0:T(8,128)(2,1)} %get-tuple-element.45), channel_id=1, source_target_pairs={{0,2},{1,3},{2,4},{3,5},{4,6},{5,7},{6,0},{7,1},{8,10},{9,11},{10,... | collective-permute-start | bytes 3145736 | tf_op jit(solution)/shard_map/ppermute | solution.py:45
  66.7 28.6 %collective-permute-start.8 = (bf16[512,1024]{1,0:T(8,128)(2,1)}, bf16[512,1024]{1,0:T(8,128)(2,1)}, u32[]{:S(2)}, u32[]{:S(2)}) collective-permute-start(bf16[512,1024]{1,0:T(8,128)(2,1)} %get-tuple-element.53), channel_id=1, source_target_pairs={{16,0},{17,1},{18,2},{19,3},{20,4},{21,5},{22,6},{23,7},{24,8},{25... | collective-permute-start | bytes 3145736 | tf_op jit(solution)/shard_map/ppermute | solution.py:45
  95.3 11.1 %collective-permute-start.11 = (bf16[528,1024]{1,0:T(8,128)(2,1)}, bf16[528,1024]{1,0:T(8,128)(2,1)}, u32[]{:S(2)}, u32[]{:S(2)}) collective-permute-start(bf16[528,1024]{1,0:T(8,128)(2,1)} %collective-permute-done.3.refs_10_), channel_id=1, source_target_pairs={{0,1},{1,0},{2,3},{3,2},{4,5},{5,4},{6,7},{7,6},{8,9},{9,8},{10,11... | collective-permute-start | bytes 3244040 | tf_op jit(solution)/shard_map/ppermute | solution.py:45
  95.3 11.1 %collective-permute-start.12 = (bf16[512,1024]{1,0:T(8,128)(2,1)}, bf16[512,1024]{1,0:T(8,128)(2,1)}, u32[]{:S(2)}, u32[]{:S(2)}) collective-permute-start(bf16[512,1024]{1,0:T(8,128)(2,1)} %collective-permute-done.2.refs_9_), channel_id=1, source_target_pairs={{0,1},{1,0},{2,3},{3,2},{4,5},{5,4},{6,7},{7,6},{8,9},{9,8},{10,11... | collective-permute-start | bytes 3145736 | tf_op jit(solution)/shard_map/ppermute | solution.py:45
  109.3 31.4 %all-to-all-start = ((f32[8,1,1024]{2,1,0:T(1,128)}), f32[8,1,1024]{2,1,0:T(1,128)S(1)}, u32[]{:S(2)}, u32[]{:S(2)}) async-start(f32[8,1,1024]{2,1,0:T(1,128)} %get-tuple-element.76), calls=%async_computation | async-start | bytes 65536 | tf_op jit(solution)/shard_map/all_to_all | solution.py:538
  123.4 11.2 %collective-permute-start.13 = (f32[1,1024]{1,0:T(1,128)}, f32[1,1024]{1,0:T(1,128)S(1)}, u32[]{:S(2)}, u32[]{:S(2)}) collective-permute-start(f32[1,1024]{1,0:T(1,128)} %get-tuple-element.77), channel_id=1, source_target_pairs={{0,8},{1,9},{2,10},{3,11},{4,12},{5,13},{6,14},{7,15},{8,16},{9,17... | collective-permute-start | bytes 12296 | tf_op jit(solution)/shard_map/ppermute | solution.py:45
  132.7 8.1 %collective-permute-start.14 = (f32[1,1024]{1,0:T(1,128)}, f32[1,1024]{1,0:T(1,128)S(1)}, u32[]{:S(2)}, u32[]{:S(2)}) collective-permute-start(f32[1,1024]{1,0:T(1,128)} %get-tuple-element.78), channel_id=1, source_target_pairs={{0,16},{1,17},{2,18},{3,19},{4,20},{5,21},{6,22},{7,23},{8,24},{9,... | collective-permute-start | bytes 12296 | tf_op jit(solution)/shard_map/ppermute | solution.py:45
  134.6 6.2 %copy-start.1 = (f32[1,1024]{1,0:T(1,128)}, f32[1,1024]{1,0:T(1,128)S(1)}, u32[]{:S(2)}) copy-start(f32[1,1024]{1,0:T(1,128)S(1)} %collective-permute-done.13.refs_0_) | copy-start | bytes 12292
  140.8 0.6 copy-start.2
  141.4 0.6 copy-start

commit v3 on v2

--- a/solution.py
+++ b/solution.py
@@ -178,9 +178,18 @@
     def used(flags):
         return functools.reduce(jnp.logical_or, [f > 0 for f in flags])
 
+    def early():
+        for c in copies(0, 0):
+            c.start()
+        for r in range(nr):
+            waited[r] = 0
+            for c in copies(1, r):
+                c.start()
+
     me = lax.axis_index("dp")
     if own_first:
         live[0, 0] = 1
+        early()
     else:
         fetched = [
             pltpu.make_async_copy(blocks[i].at[pl.ds(row, LIST), pl.ds(0, 128)], listed.at[q], list_sem.at[q])
@@ -188,6 +197,7 @@
         ]
         for copy in fetched:
             copy.start()
+        early()
         row_at = lax.broadcasted_iota(jnp.int32, (8, 128), 0)
         lane_at = lax.broadcasted_iota(jnp.int32, (8, 128), 1)
         found = jnp.zeros((8, 128), jnp.float32)
@@ -211,15 +221,6 @@
         @pl.when(need_l[q])
         def _():
             for c in copies(0, q):
-                c.start()
-
-    fetch(0)
-    for r in range(nr):
-        waited[r] = 0
-
-        @pl.when(need_r[r])
-        def _(r=r):
-            for c in copies(1, r):
                 c.start()
 
     col_f[...] = jnp.zeros_like(col_f)
@@ -384,6 +385,19 @@
         return 0
 
     lax.fori_loop(0, nl, left, 0)
+
+    @pl.when(jnp.logical_not(need_l[0]))
+    def _():
+        for c in copies(0, 0):
+            c.wait()
+
+    for r in range(nr):
+
+        @pl.when(waited[r] == 0)
+        def _(r=r):
+            for c in copies(1, r):
+                c.wait()
+
     for r in range(nr):
         col_out[r : r + 1, :] = jnp.full((1, B), FLOOR, jnp.float32)
 

time: 143 us -> 140 us (0.979); the launches traced: 143 us -> 139 us
  Pallas kernels: 34.7 us -> 48.2 us
  waiting for transfers between devices: 62.3 us -> 50.7 us
  starting transfers between devices: 44.4 us -> 37.9 us
    pallas_call x5, Pallas kernels: 26.6 us -> 40.2 us  [stage(): pl.pallas_call(functools.partial(stage_kernel, plan), out_shape=shapes, i...]
    ppermute x15, waiting for transfers between devices: 62.3 us -> 50.7 us  [send(): return lax.ppermute(value, 'dp', moves)]
    all_to_all x1, starting transfers between devices: 14.1 us -> 4.1 us  [body(): lax.all_to_all(ring_part, 'dp', 0, 0, axis_index_groups=groups, tiled=True)]
    ppermute x15, starting transfers between devices: 30.3 us -> 33.8 us  [send(): return lax.ppermute(value, 'dp', moves)]
  transfers between devices with their start and end apart: 16 -> 16, of which waited for: 6 -> 7; matrix products, arithmetic and copies ran while one was open for 0% -> 0% of each run, Pallas kernels for 18% -> 27%
where the time goes in v3:
time: 140 us; the launch traced here: 139 us
  waiting for transfers between devices  50.7 us (36%)
  Pallas kernels  48.2 us (34%)
  starting transfers between devices  37.9 us (27%)
    ppermute x15, waiting for transfers between devices, send(): return lax.ppermute(value, 'dp', moves)  50.7 us
    pallas_call x5, Pallas kernels, stage(): pl.pallas_call(functools.partial(stage_kernel, plan), out_shape=shapes, i...  40.2 us
    ppermute x15, starting transfers between devices, send(): return lax.ppermute(value, 'dp', moves)  33.8 us
    pallas_call x1, Pallas kernels, normalize(): pl.pallas_call(unit_kernel, in_specs=[smem, smem, anywhere], out_specs=[a...  4.12 us
    all_to_all x1, starting transfers between devices, body(): lax.all_to_all(ring_part, 'dp', 0, 0, axis_index_groups=groups, tiled=True)  4.1 us
  transfers between devices with their start and end apart: 16, of which 7 were waited for; matrix products, arithmetic and copies ran while one was open for 0% of the time, Pallas kernels for 27%

profile of v3, /device:TPU:34, one launch (start us, length us, event | category | flops | bytes accessed | tf_op | source)
XLA Modules:
  0.0 138.9 jit_solution(1425815430401826990)
XLA Ops:
  0.7 4.1 %unit_rows.1 = (bf16[1040,1024]{1,0:T(8,128)(2,1)}, bf16[512,1024]{1,0:T(8,128)(2,1)}, bf16[512,1024]{1,0:T(8,128)(2,1)}) custom-call(s32[1,13]{1,0:T(1,128)} %list_ref.1, s32[1]{0:T(128)S(6)} %copy.4.count_ref, bf16[1024,1024]{1,0:T(8,128)(2,1)} %x_ref.1), custom_call_target="tpu_custom_call" | custom-call | tf_op jit(solution)/shard_map/unit_rows/pallas_call | solution.py:82
  4.8 3.0 %collective-permute-start.5 = (bf16[512,1024]{1,0:T(8,128)(2,1)}, bf16[512,1024]{1,0:T(8,128)(2,1)}, u32[]{:S(2)}, u32[]{:S(2)}) collective-permute-start(bf16[512,1024]{1,0:T(8,128)(2,1)} %get-tuple-element.48), channel_id=1, source_target_pairs={{16,24},{17,25},{18,26},{19,27},{20,28},{21,29},{22,30},{23,31},{2... | collective-permute-start | bytes 3145736 | tf_op jit(solution)/shard_map/ppermute | solution.py:45
  7.8 3.6 %collective-permute-start.4 = (bf16[1040,1024]{1,0:T(8,128)(2,1)}, bf16[1040,1024]{1,0:T(8,128)(2,1)}, u32[]{:S(2)}, u32[]{:S(2)}) collective-permute-start(bf16[1040,1024]{1,0:T(8,128)(2,1)} %get-tuple-element.51.refs_0_.refs_1_.refs_5_.refs_3_.refs_11_.refs_4_), channel_id=1, source_target_pairs={{8,0},{9,1},{10,2},{11,3},{12,4},{13,5},{14,6},{15,7},{16,8},{17,9... | collective-permute-start | bytes 6389768 | tf_op jit(solution)/shard_map/ppermute | solution.py:45
  11.4 0.5 collective-permute-start.1
  11.9 1.6 %collective-permute-start = (bf16[1040,1024]{1,0:T(8,128)(2,1)}, bf16[1040,1024]{1,0:T(8,128)(2,1)}, u32[]{:S(2)}, u32[]{:S(2)}) collective-permute-start(bf16[1040,1024]{1,0:T(8,128)(2,1)} %get-tuple-element.51.refs_0_.refs_1_.refs_5_.refs_3_.refs_11_.refs_4_), channel_id=1, source_target_pairs={{0,2},{1,3},{2,4},{3,5},{4,6},{5,7},{6,0},{7,1},{8,10},{9,11},{10,... | collective-permute-start | bytes 6389768 | tf_op jit(solution)/shard_map/ppermute | solution.py:45
  13.5 6.9 %own.1 = (f32[1,1024]{1,0:T(1,128)}, f32[1,1024]{1,0:T(1,128)}) custom-call(bf16[1040,1024]{1,0:T(8,128)(2,1)} %get-tuple-element.51.refs_0_.refs_1_.refs_5_.refs_3_.refs_11_.refs_4_, bf16[1040,1024]{1,0:T(8,128)(2,1)} %get-tuple-element.51.refs_0_.refs_1_.refs_5_.refs_3_.refs_11_.refs_4_), custom_call_target="tpu_custom_call" | custom-call | flops 8589934592 | bytes 1024 | tf_op jit(solution)/shard_map/own/pallas_call | solution.py:448
  20.4 12.8 %collective-permute-done.5 = bf16[512,1024]{1,0:T(8,128)(2,1)} collective-permute-done((bf16[512,1024]{1,0:T(8,128)(2,1)}, bf16[512,1024]{1,0:T(8,128)(2,1)}, u32[]{:S(2)}, u32[]{:S(2)}) %collective-permute-start.5) | collective-permute-done | bytes 1048608 | tf_op jit(solution)/shard_map/ppermute | solution.py:45
  33.2 0.0 collective-permute-start.7
  33.2 3.1 %collective-permute-start.6 = (bf16[512,1024]{1,0:T(8,128)(2,1)}, bf16[512,1024]{1,0:T(8,128)(2,1)}, u32[]{:S(2)}, u32[]{:S(2)}) collective-permute-start(bf16[512,1024]{1,0:T(8,128)(2,1)} %collective-permute-done.5), channel_id=1, source_target_pairs={{24,0},{25,1},{26,2},{27,3},{28,4},{29,5},{30,6},{31,7},{0,8},{1,9... | collective-permute-start | bytes 3145736 | tf_op jit(solution)/shard_map/ppermute | solution.py:45
  36.3 23.1 %collective-permute-done.1.b_ref.refs_4_.refs_6_ = bf16[1040,1024]{1,0:T(8,128)(2,1)} collective-permute-done((bf16[1040,1024]{1,0:T(8,128)(2,1)}, bf16[1040,1024]{1,0:T(8,128)(2,1)}, u32[]{:S(2)}, u32[]{:S(2)}) %collective-permute-start.1) | collective-permute-done | bytes 2129952 | tf_op jit(solution)/shard_map/ppermute | solution.py:45
  59.4 1.3 collective-permute-done.a_ref.refs_3_.refs_5_
  60.7 2.5 %halves.1 = (bf16[512,1024]{1,0:T(8,128)(2,1)}, bf16[528,1024]{1,0:T(8,128)(2,1)}) custom-call(bf16[1040,1024]{1,0:T(8,128)(2,1)} %collective-permute-done.a_ref.refs_3_.refs_5_, bf16[1040,1024]{1,0:T(8,128)(2,1)} %collective-permute-done.1.b_ref.refs_4_.refs_6_), custom_call_target="tpu_custom_call" | custom-call | tf_op jit(solution)/shard_map/halves/pallas_call | solution.py:122
  63.2 0.0 collective-permute-done.6.refs_7_.refs_5_.refs_13_.refs_6_
  63.2 0.0 collective-permute-done.4.refs_6_.refs_4_.refs_12_.refs_5_
  63.2 0.0 collective-permute-done.7.refs_2_.refs_4_
  63.2 0.1 collective-permute-start.9
  63.3 0.5 collective-permute-start.10
  63.8 2.9 %collective-permute-start.3 = (bf16[528,1024]{1,0:T(8,128)(2,1)}, bf16[528,1024]{1,0:T(8,128)(2,1)}, u32[]{:S(2)}, u32[]{:S(2)}) collective-permute-start(bf16[528,1024]{1,0:T(8,128)(2,1)} %get-tuple-element.46), channel_id=1, source_target_pairs={{0,6},{1,7},{2,0},{3,1},{4,2},{5,3},{6,4},{7,5},{8,14},{9,15},{10,... | collective-permute-start | bytes 3244040 | tf_op jit(solution)/shard_map/ppermute | solution.py:45
  66.7 0.0 collective-permute-start.2
  66.7 3.4 %collective-permute-start.8 = (bf16[512,1024]{1,0:T(8,128)(2,1)}, bf16[512,1024]{1,0:T(8,128)(2,1)}, u32[]{:S(2)}, u32[]{:S(2)}) collective-permute-start(bf16[512,1024]{1,0:T(8,128)(2,1)} %get-tuple-element.53), channel_id=1, source_target_pairs={{16,0},{17,1},{18,2},{19,3},{20,4},{21,5},{22,6},{23,7},{24,8},{25... | collective-permute-start | bytes 3145736 | tf_op jit(solution)/shard_map/ppermute | solution.py:45
  70.1 14.1 %near.1 = (f32[4,1024]{1,0:T(4,128)}, f32[3,1024]{1,0:T(4,128)}) custom-call(f32[1,1024]{1,0:T(1,128)} %get-tuple-element.54.refs_0_, bf16[1040,1024]{1,0:T(8,128)(2,1)} %get-tuple-element.51.refs_0_.refs_1_.refs_5_.refs_3_.refs_11_.refs_4_, bf16[1040,1024]{1,0:T(8,128)(2,1)} %collective-permute-done.7.refs_2_.refs_4_, ...), custom_call_target="tpu_custom_call" | custom-call | flops 1024 | bytes 1024 | tf_op jit(solution)/shard_map/near/pallas_call | solution.py:448
  84.2 0.0 collective-permute-done.9.refs_1_.refs_7_
  84.2 0.0 collective-permute-done.10.refs_2_.refs_8_
  84.2 4.5 %mid.1 = (f32[2,1024]{1,0:T(2,128)}, f32[3,1024]{1,0:T(4,128)}) custom-call(f32[3,1024]{1,0:T(4,128)} %get-tuple-element.60.refs_0_, bf16[1040,1024]{1,0:T(8,128)(2,1)} %collective-permute-done.9.refs_1_.refs_7_, bf16[1040,1024]{1,0:T(8,128)(2,1)} %collective-permute-done.10.refs_2_.refs_8_, ...), custom_call_target="tpu_custom_call" | custom-call | flops 1024 | bytes 1024 | tf_op jit(solution)/shard_map/mid/pallas_call | solution.py:448
  88.7 3.2 %collective-permute-done.2.refs_9_ = bf16[512,1024]{1,0:T(8,128)(2,1)} collective-permute-done((bf16[512,1024]{1,0:T(8,128)(2,1)}, bf16[512,1024]{1,0:T(8,128)(2,1)}, u32[]{:S(2)}, u32[]{:S(2)}) %collective-permute-start.2) | collective-permute-done | bytes 1048608 | tf_op jit(solution)/shard_map/ppermute | solution.py:45
  91.9 0.0 collective-permute-done.3.refs_10_
  91.9 3.4 %collective-permute-done.8.refs_14_.refs_7_ = bf16[512,1024]{1,0:T(8,128)(2,1)} collective-permute-done((bf16[512,1024]{1,0:T(8,128)(2,1)}, bf16[512,1024]{1,0:T(8,128)(2,1)}, u32[]{:S(2)}, u32[]{:S(2)}) %collective-permute-start.8) | collective-permute-done | bytes 1048608 | tf_op jit(solution)/shard_map/ppermute | solution.py:45
  95.3 0.0 collective-permute-start.11
  95.3 0.5 collective-permute-start.12
  95.8 9.8 %far.1 = (f32[7,1024]{1,0:T(8,128)}, f32[4,1024]{1,0:T(4,128)}) custom-call(f32[4,1024]{1,0:T(4,128)} %get-tuple-element.67.refs_0_, f32[2,1024]{1,0:T(2,128)} %get-tuple-element.68.refs_1_, f32[3,1024]{1,0:T(4,128)} %get-tuple-element.69.refs_2_, bf16[1040,1024]{1,0:T(8,128)(2,1)} %get-tuple-element.51.refs_0_.refs_1_.refs_5_.refs_3_.refs_11_.refs_4_, ...), custom_call_target="tpu_custom_call" | custom-call | flops 1024 | bytes 1024 | tf_op jit(solution)/shard_map/far/pallas_call | solution.py:448
  105.6 0.0 collective-permute-done.12.refs_2_
  105.6 0.0 collective-permute-done.11.refs_3_
  105.7 4.9 %last.1 = (f32[8,1,1024]{2,1,0:T(1,128)}, f32[1,1024]{1,0:T(1,128)}, f32[1,1024]{1,0:T(1,128)}) custom-call(f32[7,1024]{1,0:T(8,128)} %get-tuple-element.72.refs_0_, f32[4,1024]{1,0:T(4,128)} %get-tuple-element.73.refs_1_, bf16[512,1024]{1,0:T(8,128)(2,1)} %collective-permute-done.12.refs_2_, bf16[528,1024]{1,0:T(8,128)(2,1)} %collective-permute-done.11.refs_3_, ...), custom_call_target="tpu_custom_call" | custom-call | flops 1024 | bytes 1024 | tf_op jit(solution)/shard_map/last/pallas_call | solution.py:448
  110.6 4.1 %all-to-all-start = ((f32[8,1,1024]{2,1,0:T(1,128)}), f32[8,1,1024]{2,1,0:T(1,128)S(1)}, u32[]{:S(2)}, u32[]{:S(2)}) async-start(f32[8,1,1024]{2,1,0:T(1,128)} %get-tuple-element.76), calls=%async_computation | async-start | bytes 65536 | tf_op jit(solution)/shard_map/all_to_all | solution.py:552
  114.7 7.7 %collective-permute-start.13 = (f32[1,1024]{1,0:T(1,128)}, f32[1,1024]{1,0:T(1,128)S(1)}, u32[]{:S(2)}, u32[]{:S(2)}) collective-permute-start(f32[1,1024]{1,0:T(1,128)} %get-tuple-element.77), channel_id=1, source_target_pairs={{0,8},{1,9},{2,10},{3,11},{4,12},{5,13},{6,14},{7,15},{8,16},{9,17... | collective-permute-start | bytes 12296 | tf_op jit(solution)/shard_map/ppermute | solution.py:45
  122.4 6.9 %collective-permute-start.14 = (f32[1,1024]{1,0:T(1,128)}, f32[1,1024]{1,0:T(1,128)S(1)}, u32[]{:S(2)}, u32[]{:S(2)}) collective-permute-start(f32[1,1024]{1,0:T(1,128)} %get-tuple-element.78), channel_id=1, source_target_pairs={{0,16},{1,17},{2,18},{3,19},{4,20},{5,21},{6,22},{7,23},{8,24},{9,... | collective-permute-start | bytes 12296 | tf_op jit(solution)/shard_map/ppermute | solution.py:45
  129.3 3.6 %collective-permute-done.13.refs_0_ = f32[1,1024]{1,0:T(1,128)S(1)} collective-permute-done((f32[1,1024]{1,0:T(1,128)}, f32[1,1024]{1,0:T(1,128)S(1)}, u32[]{:S(2)}, u32[]{:S(2)}) %collective-permute-start.13) | collective-permute-done | bytes 4128 | tf_op jit(solution)/shard_map/ppermute | solution.py:45
  132.9 0.0 copy-start.1
  132.9 3.4 %collective-permute-done.14.refs_1_ = f32[1,1024]{1,0:T(1,128)S(1)} collective-permute-done((f32[1,1024]{1,0:T(1,128)}, f32[1,1024]{1,0:T(1,128)S(1)}, u32[]{:S(2)}, u32[]{:S(2)}) %collective-permute-start.14) | collective-permute-done | bytes 4128 | tf_op jit(solution)/shard_map/ppermute | solution.py:45
  136.3 0.0 copy-start.2
  136.3 0.0 all-to-all-done.ring_ref
  136.3 0.0 copy-done.1
  136.3 0.6 copy-done.2
  136.9 0.0 copy-start
  136.9 0.6 copy-done
  137.5 1.4 %last_sum.1 = f32[1,1024]{1,0:T(1,128)} custom-call(f32[8,1,1024]{2,1,0:T(1,128)} %copy-done, f32[1,1024]{1,0:T(1,128)} %copy-done.1, f32[1,1024]{1,0:T(1,128)} %copy-done.2), custom_call_target="tpu_custom_call" | custom-call | tf_op jit(solution)/shard_map/last_sum/pallas_call | solution.py:553
Async XLA Ops:
  4.8 28.4 %collective-permute-start.5 = (bf16[512,1024]{1,0:T(8,128)(2,1)}, bf16[512,1024]{1,0:T(8,128)(2,1)}, u32[]{:S(2)}, u32[]{:S(2)}) collective-permute-start(bf16[512,1024]{1,0:T(8,128)(2,1)} %get-tuple-element.48), channel_id=1, source_target_pairs={{16,24},{17,25},{18,26},{19,27},{20,28},{21,29},{22,30},{23,31},{2... | collective-permute-start | bytes 3145736 | tf_op jit(solution)/shard_map/ppermute | solution.py:45
  7.8 55.4 %collective-permute-start.4 = (bf16[1040,1024]{1,0:T(8,128)(2,1)}, bf16[1040,1024]{1,0:T(8,128)(2,1)}, u32[]{:S(2)}, u32[]{:S(2)}) collective-permute-start(bf16[1040,1024]{1,0:T(8,128)(2,1)} %get-tuple-element.51.refs_0_.refs_1_.refs_5_.refs_3_.refs_11_.refs_4_), channel_id=1, source_target_pairs={{8,0},{9,1},{10,2},{11,3},{12,4},{13,5},{14,6},{15,7},{16,8},{17,9... | collective-permute-start | bytes 6389768 | tf_op jit(solution)/shard_map/ppermute | solution.py:45
  11.4 48.0 %collective-permute-start.1 = (bf16[1040,1024]{1,0:T(8,128)(2,1)}, bf16[1040,1024]{1,0:T(8,128)(2,1)}, u32[]{:S(2)}, u32[]{:S(2)}) collective-permute-start(bf16[1040,1024]{1,0:T(8,128)(2,1)} %get-tuple-element.51.refs_0_.refs_1_.refs_5_.refs_3_.refs_11_.refs_4_), channel_id=1, source_target_pairs={{0,6},{1,7},{2,0},{3,1},{4,2},{5,3},{6,4},{7,5},{8,14},{9,15},{10,... | collective-permute-start | bytes 6389768 | tf_op jit(solution)/shard_map/ppermute | solution.py:45
  11.9 48.7 %collective-permute-start = (bf16[1040,1024]{1,0:T(8,128)(2,1)}, bf16[1040,1024]{1,0:T(8,128)(2,1)}, u32[]{:S(2)}, u32[]{:S(2)}) collective-permute-start(bf16[1040,1024]{1,0:T(8,128)(2,1)} %get-tuple-element.51.refs_0_.refs_1_.refs_5_.refs_3_.refs_11_.refs_4_), channel_id=1, source_target_pairs={{0,2},{1,3},{2,4},{3,5},{4,6},{5,7},{6,0},{7,1},{8,10},{9,11},{10,... | collective-permute-start | bytes 6389768 | tf_op jit(solution)/shard_map/ppermute | solution.py:45
  33.2 30.0 %collective-permute-start.7 = (bf16[1040,1024]{1,0:T(8,128)(2,1)}, bf16[1040,1024]{1,0:T(8,128)(2,1)}, u32[]{:S(2)}, u32[]{:S(2)}) collective-permute-start(bf16[1040,1024]{1,0:T(8,128)(2,1)} %get-tuple-element.51.refs_0_.refs_1_.refs_5_.refs_3_.refs_11_.refs_4_), channel_id=1, source_target_pairs={{0,1},{1,0},{2,3},{3,2},{4,5},{5,4},{6,7},{7,6},{8,9},{9,8},{10,11... | collective-permute-start | bytes 6389768 | tf_op jit(solution)/shard_map/ppermute | solution.py:45
  33.2 30.0 %collective-permute-start.6 = (bf16[512,1024]{1,0:T(8,128)(2,1)}, bf16[512,1024]{1,0:T(8,128)(2,1)}, u32[]{:S(2)}, u32[]{:S(2)}) collective-permute-start(bf16[512,1024]{1,0:T(8,128)(2,1)} %collective-permute-done.5), channel_id=1, source_target_pairs={{24,0},{25,1},{26,2},{27,3},{28,4},{29,5},{30,6},{31,7},{0,8},{1,9... | collective-permute-start | bytes 3145736 | tf_op jit(solution)/shard_map/ppermute | solution.py:45
  63.2 21.0 %collective-permute-start.9 = (bf16[1040,1024]{1,0:T(8,128)(2,1)}, bf16[1040,1024]{1,0:T(8,128)(2,1)}, u32[]{:S(2)}, u32[]{:S(2)}) collective-permute-start(bf16[1040,1024]{1,0:T(8,128)(2,1)} %collective-permute-done.a_ref.refs_3_.refs_5_), channel_id=1, source_target_pairs={{0,1},{1,0},{2,3},{3,2},{4,5},{5,4},{6,7},{7,6},{8,9},{9,8},{10,11... | collective-permute-start | bytes 6389768 | tf_op jit(solution)/shard_map/ppermute | solution.py:45
  63.3 20.9 %collective-permute-start.10 = (bf16[1040,1024]{1,0:T(8,128)(2,1)}, bf16[1040,1024]{1,0:T(8,128)(2,1)}, u32[]{:S(2)}, u32[]{:S(2)}) collective-permute-start(bf16[1040,1024]{1,0:T(8,128)(2,1)} %collective-permute-done.1.b_ref.refs_4_.refs_6_), channel_id=1, source_target_pairs={{0,1},{1,0},{2,3},{3,2},{4,5},{5,4},{6,7},{7,6},{8,9},{9,8},{10,11... | collective-permute-start | bytes 6389768 | tf_op jit(solution)/shard_map/ppermute | solution.py:45
  63.8 28.1 %collective-permute-start.3 = (bf16[528,1024]{1,0:T(8,128)(2,1)}, bf16[528,1024]{1,0:T(8,128)(2,1)}, u32[]{:S(2)}, u32[]{:S(2)}) collective-permute-start(bf16[528,1024]{1,0:T(8,128)(2,1)} %get-tuple-element.46), channel_id=1, source_target_pairs={{0,6},{1,7},{2,0},{3,1},{4,2},{5,3},{6,4},{7,5},{8,14},{9,15},{10,... | collective-permute-start | bytes 3244040 | tf_op jit(solution)/shard_map/ppermute | solution.py:45
  66.7 25.2 %collective-permute-start.2 = (bf16[512,1024]{1,0:T(8,128)(2,1)}, bf16[512,1024]{1,0:T(8,128)(2,1)}, u32[]{:S(2)}, u32[]{:S(2)}) collective-permute-start(bf16[512,1024]{1,0:T(8,128)(2,1)} %get-tuple-element.45), channel_id=1, source_target_pairs={{0,2},{1,3},{2,4},{3,5},{4,6},{5,7},{6,0},{7,1},{8,10},{9,11},{10,... | collective-permute-start | bytes 3145736 | tf_op jit(solution)/shard_map/ppermute | solution.py:45
  66.7 28.6 %collective-permute-start.8 = (bf16[512,1024]{1,0:T(8,128)(2,1)}, bf16[512,1024]{1,0:T(8,128)(2,1)}, u32[]{:S(2)}, u32[]{:S(2)}) collective-permute-start(bf16[512,1024]{1,0:T(8,128)(2,1)} %get-tuple-element.53), channel_id=1, source_target_pairs={{16,0},{17,1},{18,2},{19,3},{20,4},{21,5},{22,6},{23,7},{24,8},{25... | collective-permute-start | bytes 3145736 | tf_op jit(solution)/shard_map/ppermute | solution.py:45
  95.3 10.3 %collective-permute-start.11 = (bf16[528,1024]{1,0:T(8,128)(2,1)}, bf16[528,1024]{1,0:T(8,128)(2,1)}, u32[]{:S(2)}, u32[]{:S(2)}) collective-permute-start(bf16[528,1024]{1,0:T(8,128)(2,1)} %collective-permute-done.3.refs_10_), channel_id=1, source_target_pairs={{0,1},{1,0},{2,3},{3,2},{4,5},{5,4},{6,7},{7,6},{8,9},{9,8},{10,11... | collective-permute-start | bytes 3244040 | tf_op jit(solution)/shard_map/ppermute | solution.py:45
  95.3 10.3 %collective-permute-start.12 = (bf16[512,1024]{1,0:T(8,128)(2,1)}, bf16[512,1024]{1,0:T(8,128)(2,1)}, u32[]{:S(2)}, u32[]{:S(2)}) collective-permute-start(bf16[512,1024]{1,0:T(8,128)(2,1)} %collective-permute-done.2.refs_9_), channel_id=1, source_target_pairs={{0,1},{1,0},{2,3},{3,2},{4,5},{5,4},{6,7},{7,6},{8,9},{9,8},{10,11... | collective-permute-start | bytes 3145736 | tf_op jit(solution)/shard_map/ppermute | solution.py:45
  110.6 25.8 %all-to-all-start = ((f32[8,1,1024]{2,1,0:T(1,128)}), f32[8,1,1024]{2,1,0:T(1,128)S(1)}, u32[]{:S(2)}, u32[]{:S(2)}) async-start(f32[8,1,1024]{2,1,0:T(1,128)} %get-tuple-element.76), calls=%async_computation | async-start | bytes 65536 | tf_op jit(solution)/shard_map/all_to_all | solution.py:552
  114.7 18.3 %collective-permute-start.13 = (f32[1,1024]{1,0:T(1,128)}, f32[1,1024]{1,0:T(1,128)S(1)}, u32[]{:S(2)}, u32[]{:S(2)}) collective-permute-start(f32[1,1024]{1,0:T(1,128)} %get-tuple-element.77), channel_id=1, source_target_pairs={{0,8},{1,9},{2,10},{3,11},{4,12},{5,13},{6,14},{7,15},{8,16},{9,17... | collective-permute-start | bytes 12296 | tf_op jit(solution)/shard_map/ppermute | solution.py:45
  122.4 13.9 %collective-permute-start.14 = (f32[1,1024]{1,0:T(1,128)}, f32[1,1024]{1,0:T(1,128)S(1)}, u32[]{:S(2)}, u32[]{:S(2)}) collective-permute-start(f32[1,1024]{1,0:T(1,128)} %get-tuple-element.78), channel_id=1, source_target_pairs={{0,16},{1,17},{2,18},{3,19},{4,20},{5,21},{6,22},{7,23},{8,24},{9,... | collective-permute-start | bytes 12296 | tf_op jit(solution)/shard_map/ppermute | solution.py:45
  132.9 3.4 %copy-start.1 = (f32[1,1024]{1,0:T(1,128)}, f32[1,1024]{1,0:T(1,128)S(1)}, u32[]{:S(2)}) copy-start(f32[1,1024]{1,0:T(1,128)S(1)} %collective-permute-done.13.refs_0_) | copy-start | bytes 12292
  136.3 0.6 copy-start.2
  136.9 0.6 copy-start
